TPU v7x, 512 devices: a whole 4x8x8 slice. The times are simulated.
512 devices in a mesh: dp: 64 (over y, z), tensor: 8 (over x, core).
Axes of the slice: x: 4, y: 8, z: 8, core: 2. Of those that a mesh axis runs over, the one named last changes fastest.
Arguments:
- hidden_act: bfloat16 [28672, 28672], P('dp', 'tensor'), may hold values from -160 to 160
- grad_out: bfloat16 [28672, 8192], P('dp', 'tensor'), may hold values from -160 to 160
- proj_in: bfloat16 [28672, 64], P('tensor'), may hold values from -0.03125 to 0.03125
- proj_out: bfloat16 [8192, 64], P('tensor'), may hold values from -0.0625 to 0.0625
- queries: float32 [64, 4096], P('dp'), may hold values from -6 to 6
Outputs:
- example_grads: float32 [256, 4096], P('dp')
- factor_in: float32 [64, 64], replicated
- factor_out: float32 [64, 64], replicated
- scores: float32 [256, 64], P('dp')
All inputs are finite; a program needn't handle non-finite values.
Results may differ from a plain program's by a relative error of at most 0.0003.
Values sent between devices are 32-bit elements; how exact they have to be, the bound alone decides.
No kernel may reach another device: no remote copies, remote signals or barrier semaphores. Data moves between devices by JAX's collectives and lax.ppermute only.
A program may use at most 64 MiB of HBM per device.

v0:
```python
import math

import jax
import jax.numpy as jnp
from jax import lax
from jax.sharding import PartitionSpec as P

EX_DEV = 4
TOK_EX = 112


damping_level = 0.1


def precondition(flat, chol_in, chol_out):
    item_count = flat.shape[0]
    columns = chol_in.shape[0]
    matrices = flat.reshape(item_count, columns, columns)
    stacked = matrices.transpose(1, 0, 2).reshape(columns, item_count * columns)
    solved = jax.scipy.linalg.cho_solve((chol_in, True), stacked)
    solved = (
        solved.reshape(columns, item_count, columns)
        .transpose(2, 1, 0)
        .reshape(columns, item_count * columns)
    )
    solved = jax.scipy.linalg.cho_solve((chol_out, True), solved)
    solved = solved.reshape(columns, item_count, columns).transpose(1, 2, 0)
    return solved.reshape(item_count, columns * columns)


def local(hidden_act, grad_out, proj_in, proj_out, queries):
    row_count = hidden_act.shape[0]
    columns = proj_in.shape[1]
    all_tokens = float(row_count * lax.axis_size("dp"))
    in_part = jnp.dot(hidden_act, proj_in, preferred_element_type=jnp.float32)
    out_part = jnp.dot(grad_out, proj_out, preferred_element_type=jnp.float32)
    stacked = jnp.concatenate([in_part, out_part], axis=1)
    summed = lax.psum(stacked, "tensor")
    in_proj = summed[:, :columns]
    out_proj = summed[:, columns:]
    sum_in = jnp.dot(in_proj.T, in_proj, precision=lax.Precision.HIGHEST)
    sum_out = jnp.dot(out_proj.T, out_proj, precision=lax.Precision.HIGHEST)
    sum_in, sum_out = lax.psum((sum_in, sum_out), "dp")
    in_ex = in_proj.reshape(EX_DEV, TOK_EX, columns)
    out_ex = out_proj.reshape(EX_DEV, TOK_EX, columns)
    example_grads = jnp.einsum("eti,eto->eio", in_ex, out_ex, precision=lax.Precision.HIGHEST)
    example_grads = (example_grads / math.sqrt(TOK_EX)).reshape(EX_DEV, columns * columns)
    eye_mat = jnp.eye(columns, dtype=jnp.float32)
    factor_in = sum_in / all_tokens + damping_level * eye_mat
    factor_out = sum_out / all_tokens + damping_level * eye_mat
    chol_in = jnp.linalg.cholesky(factor_in)
    chol_out = jnp.linalg.cholesky(factor_out)
    ready = precondition(queries, chol_in, chol_out)
    scores = jnp.dot(
        example_grads,
        lax.all_gather(ready, "dp", axis=0, tiled=True).T,
        precision=lax.Precision.HIGHEST,
    ) / float(columns)
    return (example_grads, factor_in, factor_out, scores)


def solution(mesh):
    placed = (
        P("dp", "tensor"),
        P("dp", "tensor"),
        P("tensor", None),
        P("tensor", None),
        P("dp", None),
    )
    return jax.shard_map(
        local,
        mesh=mesh,
        in_specs=placed,
        out_specs=(P("dp", None), P(), P(), P("dp", None)),
        check_vma=False,
    )
```

profile of v0, /device:TPU:1, one launch (start us, length us, event | category | flops | bytes accessed | tf_op | source)
XLA Modules:
  0.0 475.7 jit_solution(7794722974854268269)
XLA Ops:
  7.2 0.0 copy-start
  7.2 0.0 copy-start.4
  7.2 0.0 all-reduce.3.cloned.1.call-start
  7.2 1.7 fusion.20
  9.0 0.4 copy-done
  9.4 2.1 fusion.19
  11.5 0.7 pad_maximum_fusion
  12.2 0.0 all-reduce.3.cloned.1.call-update
  12.2 0.0 all-gather.3.cloned.1.call-start
  12.2 0.5 broadcast.85
  12.8 0.0 copy-done.4
  12.8 0.7 reduce.7
  13.4 0.1 reshape_transpose_reshape.3
  13.5 73.3 %all-reduce.3.cloned.1.call-done = f32[448,128]{0,1:T(8,128)} async-done(((f32[448,128]{0,1:T(8,128)}), f32[448,128]{0,1:T(8,128)}) %all-reduce.3.cloned.1.call-update) | async-done | bytes 229392 | tf_op jit(solution)/shard_map/psum | solution.py:38
  86.8 1.2 fusion.16
  88.1 1.2 fusion.14
  89.3 224.7 %all-reduce = (f32[64,64]{0,1:T(8,128)S(1)}, f32[64,64]{0,1:T(8,128)S(1)}) all-reduce(f32[64,64]{0,1:T(8,128)S(1)} %fusion.16, f32[64,64]{0,1:T(8,128)S(1)} %fusion.14), channel_id=1, replica_groups=mesh['dp'=64,'tensor'=8] {'dp'}, use_global_device_ids=true, to_apply=%region_1.0 | all-reduce | flops 8192 | bytes 65536 | tf_op jit(solution)/shard_map/psum | solution.py:43
  314.0 0.1 copy.33
  314.1 0.0 copy-start.2
  314.1 0.1 copy.34
  314.2 0.0 copy-start.3
  314.2 5.8 %cholesky.55 = f32[64,64]{1,0:T(8,128)S(1)} custom-call(f32[64,64]{1,0:T(8,128)S(1)} %fusion.9), custom_call_target="Cholesky" | custom-call | tf_op jit(solution)/shard_map/jit(cholesky)/cholesky | solution.py:51
  320.1 0.6 compare_reduce_fusion
  320.7 0.7 fusion.5
  321.4 4.9 %custom-call.8 = f32[1,64,64]{1,2,0:T(8,128)S(1)} custom-call(f32[1,64,64]{2,1,0:T(8,128)S(1)} %fusion.5), custom_call_target="InvertDiagBlocksLowerTriangular" | custom-call | tf_op jit(solution)/shard_map/jit(_cho_solve)/triangular_solve | solution.py:20
  326.3 0.3 fusion.7
  326.6 0.2 convolution_bitcast_fusion.1
  326.7 5.8 %cholesky.44 = f32[64,64]{1,0:T(8,128)S(1)} custom-call(f32[64,64]{1,0:T(8,128)S(1)} %fusion.13), custom_call_target="Cholesky" | custom-call | tf_op jit(solution)/shard_map/jit(cholesky)/cholesky | solution.py:52
  332.6 0.6 compare_reduce_fusion.1
  333.3 0.7 fusion.4
  333.9 4.9 %custom-call.9 = f32[1,64,64]{1,2,0:T(8,128)S(1)} custom-call(f32[1,64,64]{2,1,0:T(8,128)S(1)} %fusion.4), custom_call_target="InvertDiagBlocksLowerTriangular" | custom-call | tf_op jit(solution)/shard_map/jit(_cho_solve)/triangular_solve | solution.py:26
  338.8 0.2 fusion.11
  339.1 0.2 convolution_bitcast_fusion
  339.3 0.1 copy.32
  339.3 0.7 reshape.46
  340.0 0.0 all-gather.3.cloned.1.call-update
  340.1 1.6 fusion.18
  341.7 0.1 reshape.40
  341.8 1.0 reshape.39
  342.9 1.0 convolution_multiply_fusion
  343.9 1.0 reshape.41
  344.9 0.0 copy-start.1
  344.9 120.9 %all-gather.3.cloned.1.call-done = f32[64,1,4096]{2,1,0:T(1,128)} async-done(((f32[1,1,4096]{2,1,0:T(1,128)}), f32[64,1,4096]{2,1,0:T(1,128)}) %all-gather.3.cloned.1.call-update) | async-done | bytes 1048592 | tf_op jit(solution)/shard_map/all_gather | solution.py:56
  465.7 3.1 convolution_multiply_fusion.1
  468.9 0.0 copy-done.2
  468.9 0.0 copy-done.3
  468.9 0.0 copy-done.1
  (5 shorter events, 0.1 us)
Async XLA Ops:
  7.2 2.2 copy-start
  7.2 5.6 %copy-start.4 = (f32[1,4096]{1,0:T(1,128)S(1)}, f32[1,4096]{1,0:T(1,128)}, u32[]{:S(2)}) copy-start(f32[1,4096]{1,0:T(1,128)} %param.12) | copy-start | bytes 49156
  7.2 79.6 %all-reduce.3.cloned.1.call-start = ((), (), s32[]{:S(2)}) async-start(), calls=%async_computation | async-start | bytes 524288 | tf_op jit(solution)/shard_map/psum | solution.py:38
  12.2 453.6 %all-gather.3.cloned.1.call-start = ((), (), s32[]{:S(2)}) async-start(), calls=%async_computation.1 | async-start | bytes 1064960 | tf_op jit(solution)/shard_map/all_gather | solution.py:56
  314.1 154.8 %copy-start.2 = (f32[64,64]{1,0:T(8,128)}, f32[64,64]{1,0:T(8,128)S(1)}, u32[]{:S(2)}) copy-start(f32[64,64]{1,0:T(8,128)S(1)} %copy.33) | copy-start | bytes 49156
  314.2 154.7 %copy-start.3 = (f32[64,64]{1,0:T(8,128)}, f32[64,64]{1,0:T(8,128)S(1)}, u32[]{:S(2)}) copy-start(f32[64,64]{1,0:T(8,128)S(1)} %copy.34) | copy-start | bytes 49156
  344.9 124.0 %copy-start.1 = (f32[4,4096]{1,0:T(4,128)}, f32[4,4096]{1,0:T(4,128)S(1)}, u32[]{:S(2)}) copy-start(f32[4,4096]{1,0:T(4,128)S(1)} %reshape.41) | copy-start | bytes 196612
Sparse Core Ops, SparseCore 0:
  12.3 74.4 all-reduce.2
  340.2 125.5 all-gather.2
where the time goes:
time: 480 us; the launch traced here: 476 us
  blocking collectives  225 us (47%)
  waiting for transfers between devices  194 us (40%)
  other arithmetic  25.6 us (5%)
  between operations  14.2 us (3%)
  matrix products  11.2 us (2%)
  local copies, waits for them, and re-layouts  5.74 us (1%)
    psum x1, blocking collectives, local(): sum_in, sum_out = lax.psum((sum_in, sum_out), 'dp')  225 us
    all_gather x1, waiting for transfers between devices, local(): lax.all_gather(ready, 'dp', axis=0, tiled=True)  121 us
    psum x1, waiting for transfers between devices, local(): summed = lax.psum(stacked, 'tensor')  73.3 us
  transfers between devices with their start and end apart: 2, of which 2 were waited for; matrix products, arithmetic and copies ran while one was open for 1% of the time, Pallas kernels for 0%

commit v1 on v0

v1 whole, which is shorter than its diff:
```python
import math

import jax
import jax.numpy as jnp
from jax import lax
from jax.sharding import PartitionSpec as P

EX_DEV = 4
TOK_EX = 112
K = 64
NY = 8
NZ = 8
NT = 8


damping_level = 0.1

Y_GROUPS = [[y * NZ + z for y in range(NY)] for z in range(NZ)]
Z_GROUPS = [[y * NZ + z for z in range(NZ)] for y in range(NY)]


def swap_pairs():
    pairs = []
    for y in range(NY):
        for z in range(NZ):
            for t in range(NT):
                pairs.append(((y * NZ + z) * NT + t, (y * NZ + t) * NT + z))
    return pairs


def spread(x, count):
    return jnp.broadcast_to(x[None], (count,) + x.shape)


def local(hidden_act, grad_out, proj_in, proj_out, queries):
    row_count = hidden_act.shape[0]
    all_tokens = float(row_count * lax.axis_size("dp"))
    my_query = lax.ppermute(queries.reshape(32, 128), ("dp", "tensor"), swap_pairs())
    in_part = jnp.dot(hidden_act, proj_in, preferred_element_type=jnp.float32)
    out_part = jnp.dot(grad_out, proj_out, preferred_element_type=jnp.float32)
    part = jnp.concatenate([in_part, out_part], axis=1).reshape(NT, row_count // NT, 2 * K)
    mine = lax.all_to_all(part, "tensor", 0, 0).sum(0)
    summed = lax.all_to_all(spread(mine, NT), "tensor", 0, 0).reshape(row_count, 2 * K)
    in_proj = summed[:, :K]
    out_proj = summed[:, K:]
    sum_in = jnp.dot(in_proj.T, in_proj, precision=lax.Precision.HIGHEST)
    sum_out = jnp.dot(out_proj.T, out_proj, precision=lax.Precision.HIGHEST)
    rows = lax.broadcasted_iota(jnp.int32, (K, K), 0)
    cols = lax.broadcasted_iota(jnp.int32, (K, K), 1)
    eye_mat = jnp.eye(K, dtype=jnp.float32)
    square = jnp.where(rows >= cols, sum_in, sum_out)
    diag = jnp.sum(sum_out * eye_mat, axis=0)
    packed = jnp.concatenate(
        [
            jnp.concatenate([square[: K // 2], square[K // 2 :]], axis=1),
            jnp.broadcast_to(jnp.concatenate([diag, diag])[None], (8, 2 * K)),
        ],
        axis=0,
    )
    over_y = lax.all_to_all(
        spread(jnp.concatenate([packed, my_query], axis=0), NY),
        "dp", 0, 0, axis_index_groups=Y_GROUPS,
    )
    packed = over_y[:, :40].sum(0)
    my_queries = over_y[:, 40:]
    packed = lax.all_to_all(spread(packed, NZ), "dp", 0, 0, axis_index_groups=Z_GROUPS).sum(0)
    in_ex = in_proj.reshape(EX_DEV, TOK_EX, K)
    out_ex = out_proj.reshape(EX_DEV, TOK_EX, K)
    example_grads = jnp.einsum("eti,eto->eio", in_ex, out_ex, precision=lax.Precision.HIGHEST)
    example_grads = example_grads / math.sqrt(TOK_EX)
    square = jnp.concatenate([packed[:32, :K], packed[:32, K:]], axis=0)
    low = jnp.where(rows >= cols, square, 0.0)
    high = jnp.where(rows < cols, square, 0.0)
    sum_in = jnp.where(rows >= cols, square, low.T)
    sum_out = high + high.T + eye_mat * packed[32, :K]
    factor_in = sum_in / all_tokens + damping_level * eye_mat
    factor_out = sum_out / all_tokens + damping_level * eye_mat
    chol_in = jnp.linalg.cholesky(factor_in)
    chol_out = jnp.linalg.cholesky(factor_out)
    left = jax.scipy.linalg.cho_solve(
        (chol_in, True), example_grads.transpose(1, 0, 2).reshape(K, EX_DEV * K)
    )
    left = left.reshape(K, EX_DEV, K).transpose(2, 1, 0).reshape(K, EX_DEV * K)
    right = jax.scipy.linalg.cho_solve((chol_out, True), left)
    ready = right.reshape(K, EX_DEV, K).transpose(1, 2, 0).reshape(EX_DEV, K * K)
    part_scores = jnp.dot(
        ready, my_queries.reshape(NY, K * K).T, precision=lax.Precision.HIGHEST
    ) / float(K)
    scores = lax.all_to_all(spread(part_scores, NT), "tensor", 0, 0)
    scores = scores.transpose(1, 2, 0).reshape(EX_DEV, NY * NT)
    return (example_grads.reshape(EX_DEV, K * K), factor_in, factor_out, scores)


def solution(mesh):
    placed = (
        P("dp", "tensor"),
        P("dp", "tensor"),
        P("tensor", None),
        P("tensor", None),
        P("dp", None),
    )
    return jax.shard_map(
        local,
        mesh=mesh,
        in_specs=placed,
        out_specs=(P("dp", None), P(), P(), P("dp", None)),
        check_vma=False,
    )
```

time: 480 us -> 121 us (0.25)
  blocking collectives: 225 us -> 16.4 us
  waiting for transfers between devices: 194 us -> 21.2 us
  starting transfers between devices: 0.08 us -> 29.5 us
  between operations: 14.2 us -> 0.9 us
  local copies, waits for them, and re-layouts: 5.74 us -> 14.6 us
    psum x1 -> x0, blocking collectives: 225 us -> none  [local(): sum_in, sum_out = lax.psum((sum_in, sum_out), 'dp')]
    all_gather x1 -> x0, waiting for transfers between devices: 121 us -> none  [local(): lax.all_gather(ready, 'dp', axis=0, tiled=True)]
    psum x1 -> x0, waiting for transfers between devices: 73.3 us -> none  [local(): summed = lax.psum(stacked, 'tensor')]
    all_to_all x0 -> x4, starting transfers between devices: none -> 27.6 us  [the longest x1 13.7 us: local(): lax.all_to_all(spread(packed, NZ), 'dp', 0, 0, axis_index_groups=Z_GROUPS)]
    all_to_all x0 -> x4, waiting for transfers between devices: none -> 21.2 us  [the longest x1 10 us: local(): lax.all_to_all(spread(jnp.concatenate([packed, my_query], axis=0), NY), '...]
    all_to_all x0 -> x1, blocking collectives: none -> 16.4 us  [local(): mine = lax.all_to_all(part, 'tensor', 0, 0).sum(0)]
  transfers between devices with their start and end apart: 2 -> 5, of which waited for: 2 -> 4; matrix products, arithmetic and copies ran while one was open for 1% -> 7% of each run, Pallas kernels for 0% -> 0%
where the time goes in v1:
time: 121 us; the launch traced here: 120 us
  starting transfers between devices  29.5 us (24%)
  other arithmetic  27.4 us (23%)
  waiting for transfers between devices  21.2 us (18%)
  blocking collectives  16.4 us (14%)
  local copies, waits for them, and re-layouts  14.6 us (12%)
  matrix products  10.1 us (8%)
    all_to_all x1, blocking collectives, local(): mine = lax.all_to_all(part, 'tensor', 0, 0).sum(0)  16.4 us
    all_to_all x1, starting transfers between devices, local(): lax.all_to_all(spread(packed, NZ), 'dp', 0, 0, axis_index_groups=Z_GROUPS)  13.7 us
    all_to_all x1, waiting for transfers between devices, local(): lax.all_to_all(spread(jnp.concatenate([packed, my_query], axis=0), NY), '...  10 us
    another operation x3, other arithmetic, local(): chol_out = jnp.linalg.cholesky(factor_out)  7.27 us
    another operation x3, other arithmetic, local(): chol_in = jnp.linalg.cholesky(factor_in)  6.52 us
    another operation x2, other arithmetic, local(): right = jax.scipy.linalg.cho_solve((chol_out, True), left)  6.18 us
    another operation x2, other arithmetic, local(): jax.scipy.linalg.cho_solve((chol_in, True), example_grads.transpose(1, 0,...  5.55 us
    all_to_all x1, starting transfers between devices, local(): scores = lax.all_to_all(spread(part_scores, NT), 'tensor', 0, 0)  5.49 us
  transfers between devices with their start and end apart: 5, of which 4 were waited for; matrix products, arithmetic and copies ran while one was open for 7% of the time, Pallas kernels for 0%

profile of v1, /device:TPU:1, one launch (start us, length us, event | category | flops | bytes accessed | tf_op | source)
XLA Modules:
  0.0 120.0 jit_solution(8517658540296901582)
XLA Ops:
  0.7 1.9 %copy-done = bf16[448,3584]{1,0:T(8,128)(2,1)S(1)} copy-done((bf16[448,3584]{1,0:T(8,128)(2,1)S(1)}, bf16[448,3584]{1,0:T(8,128)(2,1)}, u32[]{:S(2)}) %copy-start) | copy-done | bytes 3211288
  2.5 2.1 %fusion.23 = f32[448,64]{0,1:T(8,128)S(1)} fusion(bf16[448,3584]{1,0:T(8,128)(2,1)S(1)} %copy-done, bf16[3584,64]{0,1:T(8,128)(2,1)} %param.10), kind=kOutput, calls=%fused_computation.49 | convolution fusion | flops 205520896 | bytes 3784704 | tf_op jit(solution)/shard_map/dot_general | solution.py:39
  4.6 0.4 fusion.24
  5.1 0.8 copy.95
  5.9 16.4 %all_to_all.25 = f32[8,56,128]{2,1,0:T(8,128)S(1)} all-to-all(f32[8,56,128]{2,1,0:T(8,128)} %bitcast.67), channel_id=1, replica_groups=mesh['dp'=64,'tensor'=8] {'tensor'}, dimensions={0} | all-to-all | bytes 458752 | tf_op jit(solution)/shard_map/all_to_all | solution.py:42
  22.3 0.7 broadcast_in_dim.12
  23.0 4.3 %all-to-all-start.1 = ((f32[8,56,128]{2,1,0:T(8,128)}), f32[8,56,128]{2,1,0:T(8,128)S(1)}, u32[]{:S(2)}, u32[]{:S(2)}) async-start(f32[8,56,128]{2,1,0:T(8,128)} %broadcast_in_dim.12), calls=%async_computation.1 | async-start | bytes 458752 | tf_op jit(solution)/shard_map/all_to_all | solution.py:43
  27.3 1.9 %collective-permute-start = (f32[32,128]{1,0:T(8,128)S(1)}, f32[32,128]{1,0:T(8,128)S(1)}, u32[]{:S(2)}, u32[]{:S(2)}) collective-permute-start(f32[32,128]{1,0:T(8,128)S(1)} %bitcast.71), channel_id=1, source_target_pairs={{0,0},{1,8},{2,16},{3,24},{4,32},{5,40},{6,48},{7,56},{8,1},{9,9},... | collective-permute-start | bytes 49160 | tf_op jit(solution)/shard_map/ppermute | solution.py:38
  29.2 4.3 %all-to-all-done.1 = f32[8,56,128]{2,1,0:T(8,128)S(1)} async-done(((f32[8,56,128]{2,1,0:T(8,128)}), f32[8,56,128]{2,1,0:T(8,128)S(1)}, u32[]{:S(2)}, u32[]{:S(2)}) %all-to-all-start.1) | async-done | bytes 229408 | tf_op jit(solution)/shard_map/all_to_all | solution.py:43
  33.5 0.7 select_reduce_fusion.2
  34.2 0.6 convolution_select_fusion
  34.9 0.7 broadcast_in_dim.14
  35.7 4.1 %all-to-all-start.2 = ((f32[8,72,128]{2,1,0:T(8,128)}), f32[8,72,128]{2,1,0:T(8,128)}, u32[]{:S(2)}, u32[]{:S(2)}) async-start(f32[8,72,128]{2,1,0:T(8,128)} %broadcast_in_dim.14), calls=%async_computation.2 | async-start | bytes 589824 | tf_op jit(solution)/shard_map/all_to_all | solution.py:60
  39.7 0.1 copy.103
  39.9 0.1 copy.104
  40.0 0.8 fusion.20
  40.8 10.0 %all-to-all-done.2 = f32[8,72,128]{2,1,0:T(8,128)} async-done(((f32[8,72,128]{2,1,0:T(8,128)}), f32[8,72,128]{2,1,0:T(8,128)}, u32[]{:S(2)}, u32[]{:S(2)}) %all-to-all-start.2) | async-done | bytes 294944 | tf_op jit(solution)/shard_map/all_to_all | solution.py:60
  50.8 0.9 slice_reduce_fusion
  51.8 0.7 broadcast_in_dim.15
  52.4 13.7 %all-to-all-start.3 = ((f32[8,40,128]{2,1,0:T(8,128)}), f32[8,40,128]{2,1,0:T(8,128)S(1)}, u32[]{:S(2)}, u32[]{:S(2)}) async-start(f32[8,40,128]{2,1,0:T(8,128)} %broadcast_in_dim.15), calls=%async_computation.3 | async-start | bytes 327680 | tf_op jit(solution)/shard_map/all_to_all | solution.py:66
  66.2 1.6 %convolution_multiply_fusion = f32[4,64,64]{2,1,0:T(8,128)S(1)} fusion(f32[4,112,64]{2,1,0:T(8,128)} %bitcast.66, f32[4,112,64]{2,1,0:T(8,128)} %bitcast.65), kind=kOutput, calls=%fused_computation | convolution fusion | flops 22036480 | bytes 294912 | tf_op jit(solution)/shard_map/eti,eto->eio/dot_general | solution.py:69
  67.8 0.7 copy.111
  68.5 1.7 %reshape.68 = f32[64,256]{1,0:T(8,128)} reshape(f32[64,4,64]{2,1,0:T(4,128)} %copy.111) | data formatting | bytes 131072 | tf_op jit(solution)/shard_map/reshape | solution.py:81
  70.2 1.6 %slice_bitcast_fusion = f32[1,8,32,128]{3,2,1,0:T(8,128)} fusion(f32[8,72,128]{2,1,0:T(8,128)} %all-to-all-done.2), kind=kLoop, calls=%fused_computation.7 | loop fusion | bytes 262144
  71.7 2.9 %all-to-all-done.3 = f32[8,40,128]{2,1,0:T(8,128)S(1)} async-done(((f32[8,40,128]{2,1,0:T(8,128)}), f32[8,40,128]{2,1,0:T(8,128)S(1)}, u32[]{:S(2)}, u32[]{:S(2)}) %all-to-all-start.3) | async-done | bytes 163872 | tf_op jit(solution)/shard_map/all_to_all | solution.py:66
  75.5 0.6 fusion.8
  76.1 5.8 %cholesky.55 = f32[64,64]{1,0:T(8,128)S(1)} custom-call(f32[64,64]{1,0:T(8,128)S(1)} %get-tuple-element.42), custom_call_target="Cholesky" | custom-call | tf_op jit(solution)/shard_map/jit(cholesky)/cholesky | solution.py:78
  82.0 0.6 compare_reduce_fusion
  82.6 0.7 fusion.3
  83.3 4.9 %custom-call.8 = f32[1,64,64]{1,2,0:T(8,128)S(1)} custom-call(f32[1,64,64]{2,1,0:T(8,128)S(1)} %fusion.3), custom_call_target="InvertDiagBlocksLowerTriangular" | custom-call | tf_op jit(solution)/shard_map/jit(_cho_solve)/triangular_solve | solution.py:80
  88.2 1.1 fusion.6
  89.3 0.2 fusion.4
  89.5 6.6 %cholesky.44 = f32[64,64]{1,0:T(8,128)S(1)} custom-call(f32[64,64]{1,0:T(8,128)} %get-tuple-element.43), custom_call_target="Cholesky" | custom-call | tf_op jit(solution)/shard_map/jit(cholesky)/cholesky | solution.py:79
  96.1 0.6 compare_reduce_fusion.1
  96.8 0.7 fusion.2
  97.4 5.5 %custom-call.9 = f32[1,64,64]{1,2,0:T(8,128)} custom-call(f32[1,64,64]{2,1,0:T(8,128)S(1)} %fusion.2), custom_call_target="InvertDiagBlocksLowerTriangular" | custom-call | tf_op jit(solution)/shard_map/jit(_cho_solve)/triangular_solve | solution.py:84
  103.0 0.1 reshape.69
  103.1 0.7 copy.112
  103.8 1.0 reshape.70
  104.9 1.0 fusion.11
  105.9 1.2 fusion.9
  107.0 0.1 reshape.72
  107.1 1.3 %convolution_multiply_fusion.1 = f32[4,8]{1,0:T(4,128)S(1)} fusion(f32[4,4096]{1,0:T(4,128)S(1)} %reshape.72, f32[1,8,32,128]{3,2,1,0:T(8,128)} %slice_bitcast_fusion), kind=kOutput, calls=%fused_computation.2 | convolution fusion | flops 1572896 | bytes 196736 | tf_op jit(solution)/shard_map/dot_general | solution.py:86
  108.4 0.6 broadcast_in_dim.16
  109.1 5.5 %all-to-all-start.4 = ((f32[8,4,8]{2,1,0:T(4,128)}), f32[8,4,8]{2,1,0:T(4,128)S(1)}, u32[]{:S(2)}, u32[]{:S(2)}) async-start(f32[8,4,8]{2,1,0:T(4,128)} %broadcast_in_dim.16), calls=%async_computation.4 | async-start | bytes 32768 | tf_op jit(solution)/shard_map/all_to_all | solution.py:89
  114.6 0.7 reshape.66
  115.3 3.9 %all-to-all-done.4 = f32[8,4,8]{2,1,0:T(4,128)S(1)} async-done(((f32[8,4,8]{2,1,0:T(4,128)}), f32[8,4,8]{2,1,0:T(4,128)S(1)}, u32[]{:S(2)}, u32[]{:S(2)}) %all-to-all-start.4) | async-done | bytes 1056 | tf_op jit(solution)/shard_map/all_to_all | solution.py:89
  119.3 0.7 reshape.74
  (36 shorter events, 1.1 us)
Async XLA Ops:
  0.6 1.9 %copy-start = (bf16[448,3584]{1,0:T(8,128)(2,1)S(1)}, bf16[448,3584]{1,0:T(8,128)(2,1)}, u32[]{:S(2)}) copy-start(bf16[448,3584]{1,0:T(8,128)(2,1)} %param.8) | copy-start | bytes 9633796
  0.6 4.0 %copy-start.2 = (bf16[1024,64]{0,1:T(8,128)(2,1)S(1)}, bf16[1024,64]{0,1:T(8,128)(2,1)}, u32[]{:S(2)}) copy-start(bf16[1024,64]{0,1:T(8,128)(2,1)} %param.11) | copy-start | bytes 393220
  0.7 4.0 %copy-start.1 = (bf16[448,1024]{1,0:T(8,128)(2,1)S(1)}, bf16[448,1024]{1,0:T(8,128)(2,1)}, u32[]{:S(2)}) copy-start(bf16[448,1024]{1,0:T(8,128)(2,1)} %param.9) | copy-start | bytes 2752516
  2.5 24.7 %copy-start.5 = (f32[1,4096]{1,0:T(1,128)S(1)}, f32[1,4096]{1,0:T(1,128)}, u32[]{:S(2)}) copy-start(f32[1,4096]{1,0:T(1,128)} %param.12) | copy-start | bytes 49156
  23.0 10.5 %all-to-all-start.1 = ((f32[8,56,128]{2,1,0:T(8,128)}), f32[8,56,128]{2,1,0:T(8,128)S(1)}, u32[]{:S(2)}, u32[]{:S(2)}) async-start(f32[8,56,128]{2,1,0:T(8,128)} %broadcast_in_dim.12), calls=%async_computation.1 | async-start | bytes 458752 | tf_op jit(solution)/shard_map/all_to_all | solution.py:43
  27.3 7.6 %collective-permute-start = (f32[32,128]{1,0:T(8,128)S(1)}, f32[32,128]{1,0:T(8,128)S(1)}, u32[]{:S(2)}, u32[]{:S(2)}) collective-permute-start(f32[32,128]{1,0:T(8,128)S(1)} %bitcast.71), channel_id=1, source_target_pairs={{0,0},{1,8},{2,16},{3,24},{4,32},{5,40},{6,48},{7,56},{8,1},{9,9},... | collective-permute-start | bytes 49160 | tf_op jit(solution)/shard_map/ppermute | solution.py:38
  35.7 15.2 %all-to-all-start.2 = ((f32[8,72,128]{2,1,0:T(8,128)}), f32[8,72,128]{2,1,0:T(8,128)}, u32[]{:S(2)}, u32[]{:S(2)}) async-start(f32[8,72,128]{2,1,0:T(8,128)} %broadcast_in_dim.14), calls=%async_computation.2 | async-start | bytes 589824 | tf_op jit(solution)/shard_map/all_to_all | solution.py:60
  52.4 22.2 %all-to-all-start.3 = ((f32[8,40,128]{2,1,0:T(8,128)}), f32[8,40,128]{2,1,0:T(8,128)S(1)}, u32[]{:S(2)}, u32[]{:S(2)}) async-start(f32[8,40,128]{2,1,0:T(8,128)} %broadcast_in_dim.15), calls=%async_computation.3 | async-start | bytes 327680 | tf_op jit(solution)/shard_map/all_to_all | solution.py:66
  75.4 0.7 copy-start.3
  75.4 22.0 %copy-start.4 = (f32[64,64]{1,0:T(8,128)}, f32[64,64]{1,0:T(8,128)S(1)}, u32[]{:S(2)}) copy-start(f32[64,64]{1,0:T(8,128)S(1)} %copy.115) | copy-start | bytes 49156
  109.1 10.2 %all-to-all-start.4 = ((f32[8,4,8]{2,1,0:T(4,128)}), f32[8,4,8]{2,1,0:T(4,128)S(1)}, u32[]{:S(2)}, u32[]{:S(2)}) async-start(f32[8,4,8]{2,1,0:T(4,128)} %broadcast_in_dim.16), calls=%async_computation.4 | async-start | bytes 32768 | tf_op jit(solution)/shard_map/all_to_all | solution.py:89

commit v2 on v0

v2 whole, which is shorter than its diff:
```python
import functools
import math

import jax
import jax.numpy as jnp
from jax import lax
from jax.experimental import pallas as pl
from jax.experimental.pallas import tpu as pltpu
from jax.sharding import PartitionSpec as P

EX_DEV = 4
TOK_EX = 112
K = 64
NQ = 64
NY = 8
NZ = 8
NT = 8
GRAM = 40
ROWS = 56
QROWS = 32
UNIT_BLOCKS = (1280, 1280, 1024)
HI = lax.Precision.HIGHEST
F32 = jnp.float32
VMEM_LIMIT = 16 << 20
WIDE_VMEM_LIMIT = 60 << 20


damping_level = 0.1

Y_GROUPS = [[y * NZ + z for y in range(NY)] for z in range(NZ)]
Z_GROUPS = [[y * NZ + z for z in range(NZ)] for y in range(NY)]


def swap_pairs():
    pairs = []
    for y in range(NY):
        for z in range(NZ):
            for t in range(NT):
                pairs.append(((y * NZ + z) * NT + t, (y * NZ + t) * NT + z))
    return pairs


def gauss_jordan(m, panel):
    lane = lax.broadcasted_iota(jnp.int32, (K, 2 * K), 1)
    half = lane & K
    col_of = lane & (K - 1)
    sub = lax.broadcasted_iota(jnp.int32, (K, 2 * K), 0)
    for first in range(0, K, panel):
        cols = [jnp.take_along_axis(m, half + k, axis=1) for k in range(first, first + panel)]
        for k in range(first, first + panel):
            c = cols[k - first]
            inv = 1.0 / c[k : k + 1]
            row = jnp.where(col_of[:1] == k, 1.0, m[k : k + 1]) * inv
            for j in range(k + 1, first + panel):
                d = cols[j - first]
                f = d[k : k + 1] * inv
                cols[j - first] = jnp.where(sub == k, f, d - c * f)
            m = jnp.where(sub == k, row, jnp.where(col_of == k, 0.0, m) - c * row)
    return m


def call(body, outs, *args, scratch=(), flops=1 << 20):
    return pl.pallas_call(
        body,
        out_shape=[jax.ShapeDtypeStruct(shape, F32) for shape in outs],
        scratch_shapes=[pltpu.VMEM(shape, F32) for shape in scratch],
        compiler_params=pltpu.CompilerParams(vmem_limit_bytes=VMEM_LIMIT),
        cost_estimate=pl.CostEstimate(flops=flops, bytes_accessed=1 << 20, transcendentals=0),
    )(*args)


def added(ref, rows):
    total = ref[0, rows]
    for i in range(1, ref.shape[0]):
        total = total + ref[i, rows]
    return total


def project_kernel(hidden_ref, grad_ref, win_ref, wout_ref, out_ref, hidden, grad, win, wout, sems):
    contract = (((1,), (1,)), ((), ()))
    wout_copy = pltpu.make_async_copy(wout_ref, wout, sems.at[0])
    grad_copy = pltpu.make_async_copy(grad_ref, grad, sems.at[1])
    win_copy = pltpu.make_async_copy(win_ref, win, sems.at[2])
    wout_copy.start()
    grad_copy.start()
    win_copy.start()
    blocks = []
    first = 0
    for i, size in enumerate(UNIT_BLOCKS):
        units = pl.ds(first, size)
        copy = pltpu.make_async_copy(hidden_ref.at[:, units], hidden.at[:, units], sems.at[3 + i])
        copy.start()
        blocks.append((copy, units))
        first += size
    wout_copy.wait()
    grad_copy.wait()
    out_part = lax.dot_general(grad[...], wout[...], contract, preferred_element_type=F32)
    win_copy.wait()
    in_part = None
    for copy, units in blocks:
        copy.wait()
        part = lax.dot_general(hidden[:, units], win[:, units], contract, preferred_element_type=F32)
        in_part = part if in_part is None else in_part + part
    out_ref[:, :, :K] = in_part.reshape(NT, ROWS, K)
    out_ref[:, :, K:] = out_part.reshape(NT, ROWS, K)


def project(hidden_act, grad_out, proj_in, proj_out):
    operands = (hidden_act, grad_out, proj_in.T, proj_out.T)
    return pl.pallas_call(
        project_kernel,
        in_specs=[pl.BlockSpec(memory_space=pltpu.HBM)] * len(operands),
        out_shape=jax.ShapeDtypeStruct((NT, ROWS, 2 * K), F32),
        scratch_shapes=[pltpu.VMEM(x.shape, x.dtype) for x in operands]
        + [pltpu.SemaphoreType.DMA((3 + len(UNIT_BLOCKS),))],
        compiler_params=pltpu.CompilerParams(vmem_limit_bytes=WIDE_VMEM_LIMIT),
    )(*operands)


def rows_kernel(parts_ref, query_ref, send_ref, kept_ref):
    mine = added(parts_ref, pl.ds(0, ROWS))
    for t in range(NT):
        send_ref[t] = mine
    kept_ref[...] = query_ref[...]


def gram_kernel(rows_ref, query_ref, send_ref, wide_ref):
    gram = jnp.zeros((2 * K, 2 * K), F32)
    for e in range(EX_DEV):
        rows = rows_ref[2 * e : 2 * e + 2].reshape(TOK_EX, 2 * K)
        product = lax.dot_general(
            rows, rows, (((0,), (0,)), ((), ())), precision=HI, preferred_element_type=F32
        )
        gram = gram + product
        pair, side = divmod(e, 2)
        grad = product[:K, K:] / math.sqrt(TOK_EX)
        wide_ref[pair * K : (pair + 1) * K, side * K : (side + 1) * K] = grad
    packed = pack(gram[:K, :K], gram[K:, K:])
    query = query_ref[...]
    for y in range(NY):
        send_ref[y, :GRAM] = packed
        send_ref[y, GRAM:] = query


def over_y_kernel(parts_ref, send_ref):
    packed = added(parts_ref, pl.ds(0, GRAM))
    for z in range(NZ):
        send_ref[z] = packed


def pack(square_in, square_out):
    rows = lax.broadcasted_iota(jnp.int32, (K, K), 0)
    cols = lax.broadcasted_iota(jnp.int32, (K, K), 1)
    square = jnp.where(rows >= cols, square_in, square_out)
    diag = jnp.sum(jnp.where(rows == cols, square_out, 0.0), axis=0, keepdims=True)
    diag = jnp.broadcast_to(jnp.concatenate([diag, diag], axis=1), (8, 2 * K))
    return jnp.concatenate(
        [jnp.concatenate([square[: K // 2], square[K // 2 :]], axis=1), diag], axis=0
    )

def unpack(packed):
    rows = lax.broadcasted_iota(jnp.int32, (K, K), 0)
    cols = lax.broadcasted_iota(jnp.int32, (K, K), 1)
    square = jnp.concatenate([packed[: K // 2, :K], packed[: K // 2, K:]], axis=0)
    flipped = square.T
    square_in = jnp.where(rows >= cols, square, flipped)
    square_out = jnp.where(rows < cols, square, flipped)
    square_out = jnp.where(rows == cols, packed[K // 2 : K // 2 + 1, :K], square_out)
    return square_in, square_out

def wide_rows(wide_ref):
    blocks = []
    for pair in range(2):
        even = wide_ref[pl.ds(pair * K, K // 2, stride=2), :]
        odd = wide_ref[pl.ds(pair * K + 1, K // 2, stride=2), :]
        blocks.append(jnp.concatenate([even[:, :K], odd[:, :K]], axis=1))
        blocks.append(jnp.concatenate([even[:, K:], odd[:, K:]], axis=1))
    return blocks


def tail_kernel(all_tokens, parts_ref, grads_ref, query_ref, factors_ref, send_ref, wide_ref):
    sum_in, sum_out = unpack(added(parts_ref, pl.ds(0, GRAM)))
    rows = lax.broadcasted_iota(jnp.int32, (K, 2 * K), 0)
    cols = lax.broadcasted_iota(jnp.int32, (K, 2 * K), 1)
    eye_mats = jnp.where(rows == (cols & (K - 1)), 1.0, 0.0)
    factors = jnp.concatenate([sum_in, sum_out], axis=1) / all_tokens + damping_level * eye_mats
    factors_ref[...] = factors
    inverse = gauss_jordan(factors, 8)
    in_inv = inverse[:, :K]
    out_inv = inverse[:, K:] / float(K)
    zero = jnp.zeros((K, K), F32)
    pair_inv = jnp.concatenate(
        [jnp.concatenate([out_inv, zero], axis=1), jnp.concatenate([zero, out_inv], axis=1)], axis=0
    )
    for pair in range(2):
        left = jnp.dot(
            in_inv, grads_ref[pair * K : (pair + 1) * K], precision=HI, preferred_element_type=F32
        )
        wide_ref[pair * K : (pair + 1) * K] = jnp.dot(
            left, pair_inv, precision=HI, preferred_element_type=F32
        )
    ready = wide_rows(wide_ref)
    sums = [jnp.zeros((NY, 2 * K), F32) for _ in range(EX_DEV)]
    for r in range(QROWS):
        block = query_ref[pl.ds(GRAM + r, NY, stride=GRAM + QROWS), :]
        for e in range(EX_DEV):
            sums[e] = sums[e] + block * ready[e][r : r + 1]
    total = lax.dot_general(
        jnp.ones((8, 2 * K), F32),
        jnp.concatenate(sums, axis=0),
        (((1,), (1,)), ((), ())),
        precision=HI,
        preferred_element_type=F32,
    )
    source = lax.broadcasted_iota(jnp.int32, (EX_DEV * NY, EX_DEV * NQ), 0)
    target = lax.broadcasted_iota(jnp.int32, (EX_DEV * NY, EX_DEV * NQ), 1)
    place = jnp.where(source * NZ + lax.axis_index("tensor") == target, 1.0, 0.0)
    placed = jnp.dot(total, place, precision=HI, preferred_element_type=F32)
    for t in range(NT):
        send_ref[t] = placed[:1]


def last_kernel(parts_ref, factors_ref, wide_ref, grads_ref, fin_ref, fout_ref, scores_ref, tall_ref):
    total = added(parts_ref, pl.ds(0, 1))
    for e in range(EX_DEV):
        scores_ref[e : e + 1, :] = total[:, e * NQ : (e + 1) * NQ]
    fin_ref[...] = factors_ref[:, :K]
    fout_ref[...] = factors_ref[:, K:]
    for e, block in enumerate(wide_rows(wide_ref)):
        tall_ref[e * QROWS : (e + 1) * QROWS] = block
    for r in range(QROWS):
        grads_ref[:, r * 2 * K : (r + 1) * 2 * K] = tall_ref[pl.ds(r, EX_DEV, stride=QROWS), :]


def local(hidden_act, grad_out, proj_in, proj_out, queries):
    all_tokens = float(hidden_act.shape[0] * lax.axis_size("dp"))
    query = lax.ppermute(queries.reshape(QROWS, 2 * K), ("dp", "tensor"), swap_pairs())
    part = project(hidden_act, grad_out, proj_in, proj_out)
    parts = lax.all_to_all(part, "tensor", 0, 0)
    send, query = call(rows_kernel, [(NT, ROWS, 2 * K), (QROWS, 2 * K)], parts, query)
    rows = lax.all_to_all(send, "tensor", 0, 0)
    send, wide = call(gram_kernel, [(NY, GRAM + QROWS, 2 * K), (2 * K, 2 * K)], rows, query)
    over_y = lax.all_to_all(send, "dp", 0, 0, axis_index_groups=Y_GROUPS)
    (send,) = call(over_y_kernel, [(NZ, GRAM, 2 * K)], over_y)
    parts = lax.all_to_all(send, "dp", 0, 0, axis_index_groups=Z_GROUPS)
    factors, send = call(
        functools.partial(tail_kernel, all_tokens),
        [(K, 2 * K), (NT, 1, EX_DEV * NQ)],
        parts,
        wide,
        over_y.reshape(NY * (GRAM + QROWS), 2 * K),
        scratch=[(2 * K, 2 * K)],
    )
    parts = lax.all_to_all(send, "tensor", 0, 0)
    return tuple(
        call(
            last_kernel,
            [(EX_DEV, K * K), (K, K), (K, K), (EX_DEV, NQ)],
            parts,
            factors,
            wide,
            scratch=[(EX_DEV * QROWS, 2 * K)],
        )
    )


def solution(mesh):
    placed = (
        P("dp", "tensor"),
        P("dp", "tensor"),
        P("tensor", None),
        P("tensor", None),
        P("dp", None),
    )
    return jax.shard_map(
        local,
        mesh=mesh,
        in_specs=placed,
        out_specs=(P("dp", None), P(), P(), P("dp", None)),
        check_vma=False,
    )
```

time: 480 us -> 83.6 us (0.17)
  waiting for transfers between devices: 194 us -> 4.3 us
  blocking collectives: 225 us -> 57.3 us
  other arithmetic: 25.6 us -> 0 us
  between operations: 14.2 us -> 0.67 us
  starting transfers between devices: 0.08 us -> 12.1 us
  matrix products: 11.2 us -> 0 us
  Pallas kernels: 0 us -> 8.84 us
  local copies, waits for them, and re-layouts: 5.74 us -> 0.01 us
    psum x1 -> x0, blocking collectives: 225 us -> none  [local(): sum_in, sum_out = lax.psum((sum_in, sum_out), 'dp')]
    all_gather x1 -> x0, waiting for transfers between devices: 121 us -> none  [local(): lax.all_gather(ready, 'dp', axis=0, tiled=True)]
    psum x1 -> x0, waiting for transfers between devices: 73.3 us -> none  [local(): summed = lax.psum(stacked, 'tensor')]
    all_to_all x0 -> x4, blocking collectives: none -> 57.3 us  [the longest x1 16.5 us: local(): rows = lax.all_to_all(send, 'tensor', 0, 0)]
    another operation x10 -> x0, other arithmetic: 24.1 us -> none  [the longest x3 6.52 us: local(): chol_in = jnp.linalg.cholesky(factor_in)]
    dot_general x6 -> x0, matrix products: 10.4 us -> none  [the longest x1 3.13 us: local(): jnp.dot(example_grads, lax.all_gather(ready, 'dp', axis=0, tiled=True).T,...]
    all_to_all x0 -> x1, starting transfers between devices: none -> 10.2 us  [local(): parts = lax.all_to_all(part, 'tensor', 0, 0)]
    pallas_call x0 -> x6, Pallas kernels: none -> 8.84 us  [the longest x5 4.67 us: call(): pl.pallas_call(body, out_shape=[jax.ShapeDtypeStruct(shape, F32) for shap...]
  transfers between devices with their start and end apart: 2 -> 2, of which waited for: 2 -> 2; matrix products, arithmetic and copies ran while one was open for 1% -> 0% of each run, Pallas kernels for 0% -> 0%
where the time goes in v2:
time: 83.6 us; the launch traced here: 83.2 us
  blocking collectives  57.3 us (69%)
  starting transfers between devices  12.1 us (14%)
  Pallas kernels  8.84 us (11%)
  waiting for transfers between devices  4.3 us (5%)
    all_to_all x1, blocking collectives, local(): rows = lax.all_to_all(send, 'tensor', 0, 0)  16.5 us
    all_to_all x1, blocking collectives, local(): parts = lax.all_to_all(send, 'dp', 0, 0, axis_index_groups=Z_GROUPS)  16.4 us
    all_to_all x1, blocking collectives, local(): over_y = lax.all_to_all(send, 'dp', 0, 0, axis_index_groups=Y_GROUPS)  13.1 us
    all_to_all x1, blocking collectives, local(): parts = lax.all_to_all(send, 'tensor', 0, 0)  11.3 us
    all_to_all x1, starting transfers between devices, local(): parts = lax.all_to_all(part, 'tensor', 0, 0)  10.2 us
    pallas_call x5, Pallas kernels, call(): pl.pallas_call(body, out_shape=[jax.ShapeDtypeStruct(shape, F32) for shap...  4.67 us
    pallas_call x1, Pallas kernels, project(): pl.pallas_call(project_kernel, in_specs=[pl.BlockSpec(memory_space=pltpu....  4.17 us
    ppermute x1, waiting for transfers between devices, local(): lax.ppermute(queries.reshape(QROWS, 2 * K), ('dp', 'tensor'), swap_pairs())  3.42 us
  transfers between devices with their start and end apart: 2, of which 2 were waited for; matrix products, arithmetic and copies ran while one was open for 0% of the time, Pallas kernels for 0%

profile of v2, /device:TPU:1, one launch (start us, length us, event | category | flops | bytes accessed | tf_op | source)
XLA Modules:
  0.0 83.2 jit_solution(15408948432776496321)
XLA Ops:
  0.6 0.0 copy-start
  0.6 4.2 %shard_map.84 = f32[8,56,128]{2,1,0:T(8,128)} custom-call(bf16[448,3584]{1,0:T(8,128)(2,1)} %hidden_ref.1, bf16[448,1024]{1,0:T(8,128)(2,1)} %grad_ref.1, bf16[64,3584]{1,0:T(8,128)(2,1)} %bitcast.5, bf16[64,1024]{1,0:T(8,128)(2,1)} %bitcast.6), custom_call_target="tpu_custom_call" | custom-call | tf_op jit(solution)/shard_map/pallas_call | solution.py:110
  4.8 10.2 %all-to-all-start = ((f32[8,56,128]{2,1,0:T(8,128)}), f32[8,56,128]{2,1,0:T(8,128)S(1)}, u32[]{:S(2)}, u32[]{:S(2)}) async-start(f32[8,56,128]{2,1,0:T(8,128)} %shard_map.84), calls=%async_computation | async-start | bytes 458752 | tf_op jit(solution)/shard_map/all_to_all | solution.py:239
  15.0 0.0 copy-done
  15.0 1.9 %collective-permute-start = (f32[32,128]{1,0:T(8,128)S(1)}, f32[32,128]{1,0:T(8,128)S(1)}, u32[]{:S(2)}, u32[]{:S(2)}) collective-permute-start(f32[32,128]{1,0:T(8,128)S(1)} %bitcast.7), channel_id=1, source_target_pairs={{0,0},{1,8},{2,16},{3,24},{4,32},{5,40},{6,48},{7,56},{8,1},{9,9},... | collective-permute-start | bytes 49160 | tf_op jit(solution)/shard_map/ppermute | solution.py:237
  16.9 3.4 %collective-permute-done.query_ref = f32[32,128]{1,0:T(8,128)S(1)} collective-permute-done((f32[32,128]{1,0:T(8,128)S(1)}, f32[32,128]{1,0:T(8,128)S(1)}, u32[]{:S(2)}, u32[]{:S(2)}) %collective-permute-start) | collective-permute-done | bytes 16416 | tf_op jit(solution)/shard_map/ppermute | solution.py:237
  20.4 0.9 %all-to-all-done.parts_ref = f32[8,56,128]{2,1,0:T(8,128)S(1)} async-done(((f32[8,56,128]{2,1,0:T(8,128)}), f32[8,56,128]{2,1,0:T(8,128)S(1)}, u32[]{:S(2)}, u32[]{:S(2)}) %all-to-all-start) | async-done | bytes 229408 | tf_op jit(solution)/shard_map/all_to_all | solution.py:239
  21.3 16.5 %all_to_all.25.rows_ref = f32[8,56,128]{2,1,0:T(8,128)S(1)} all-to-all(f32[8,56,128]{2,1,0:T(8,128)S(1)} %get-tuple-element.10), channel_id=1, replica_groups=mesh['dp'=64,'tensor'=8] {'tensor'}, dimensions={0} | all-to-all | bytes 458752 | tf_op jit(solution)/shard_map/all_to_all | solution.py:241
  37.8 0.6 shard_map.86
  38.4 13.1 %all_to_all.26.parts_ref = f32[8,72,128]{2,1,0:T(8,128)S(1)} all-to-all(f32[8,72,128]{2,1,0:T(8,128)S(1)} %get-tuple-element.12), channel_id=1, replica_groups={{0,64,128,192,256,320,384,448},{8,72,136,200,264,328,392,456},{16,80,14..., dimensions={0} | all-to-all | bytes 589824 | tf_op jit(solution)/shard_map/all_to_all | solution.py:243
  51.4 16.4 %all_to_all.27.parts_ref = f32[8,40,128]{2,1,0:T(8,128)S(1)} all-to-all(f32[8,40,128]{2,1,0:T(8,128)S(1)} %shard_map.87), channel_id=1, replica_groups={{0,8,16,24,32,40,48,56},{64,72,80,88,96,104,112,120},{128,136,144,152,1..., dimensions={0} | all-to-all | bytes 327680 | tf_op jit(solution)/shard_map/all_to_all | solution.py:245
  67.9 3.3 %shard_map.88 = (f32[64,128]{1,0:T(8,128)S(1)}, f32[8,1,256]{2,1,0:T(1,128)S(1)}) custom-call(f32[8,40,128]{2,1,0:T(8,128)S(1)} %all_to_all.27.parts_ref, f32[128,128]{1,0:T(8,128)S(1)} %get-tuple-element.13.grads_ref.wide_ref, f32[576,128]{1,0:T(8,128)S(1)} %bitcast.4), custom_call_target="tpu_custom_call" | custom-call | flops 1048576 | bytes 1048576 | tf_op jit(solution)/shard_map/pallas_call | solution.py:63
  71.2 11.3 %all_to_all.28.parts_ref = f32[8,1,256]{2,1,0:T(1,128)S(1)} all-to-all(f32[8,1,256]{2,1,0:T(1,128)S(1)} %get-tuple-element.14), channel_id=1, replica_groups=mesh['dp'=64,'tensor'=8] {'tensor'}, dimensions={0} | all-to-all | bytes 16384 | tf_op jit(solution)/shard_map/all_to_all | solution.py:254
  82.4 0.8 shard_map.89
  (2 shorter events, 0.0 us)
Async XLA Ops:
  0.6 14.4 %copy-start = (f32[1,4096]{1,0:T(1,128)S(1)}, f32[1,4096]{1,0:T(1,128)}, u32[]{:S(2)}) copy-start(f32[1,4096]{1,0:T(1,128)} %param.9) | copy-start | bytes 49156
  4.8 16.4 %all-to-all-start = ((f32[8,56,128]{2,1,0:T(8,128)}), f32[8,56,128]{2,1,0:T(8,128)S(1)}, u32[]{:S(2)}, u32[]{:S(2)}) async-start(f32[8,56,128]{2,1,0:T(8,128)} %shard_map.84), calls=%async_computation | async-start | bytes 458752 | tf_op jit(solution)/shard_map/all_to_all | solution.py:239
  15.0 5.3 %collective-permute-start = (f32[32,128]{1,0:T(8,128)S(1)}, f32[32,128]{1,0:T(8,128)S(1)}, u32[]{:S(2)}, u32[]{:S(2)}) collective-permute-start(f32[32,128]{1,0:T(8,128)S(1)} %bitcast.7), channel_id=1, source_target_pairs={{0,0},{1,8},{2,16},{3,24},{4,32},{5,40},{6,48},{7,56},{8,1},{9,9},... | collective-permute-start | bytes 49160 | tf_op jit(solution)/shard_map/ppermute | solution.py:237

commit v3 on v2

--- a/solution.py
+++ b/solution.py
@@ -18,6 +18,7 @@
 GRAM = 40
 ROWS = 56
 QROWS = 32
+SLICE = QROWS // NT
 UNIT_BLOCKS = (1280, 1280, 1024)
 HI = lax.Precision.HIGHEST
 F32 = jnp.float32
@@ -29,15 +30,6 @@
 
 Y_GROUPS = [[y * NZ + z for y in range(NY)] for z in range(NZ)]
 Z_GROUPS = [[y * NZ + z for z in range(NZ)] for y in range(NY)]
-
-
-def swap_pairs():
-    pairs = []
-    for y in range(NY):
-        for z in range(NZ):
-            for t in range(NT):
-                pairs.append(((y * NZ + z) * NT + t, (y * NZ + t) * NT + z))
-    return pairs
 
 
 def gauss_jordan(m, panel):
@@ -117,11 +109,10 @@
     )(*operands)
 
 
-def rows_kernel(parts_ref, query_ref, send_ref, kept_ref):
+def rows_kernel(parts_ref, send_ref):
     mine = added(parts_ref, pl.ds(0, ROWS))
     for t in range(NT):
         send_ref[t] = mine
-    kept_ref[...] = query_ref[...]
 
 
 def gram_kernel(rows_ref, query_ref, send_ref, wide_ref):
@@ -135,27 +126,28 @@
         pair, side = divmod(e, 2)
         grad = product[:K, K:] / math.sqrt(TOK_EX)
         wide_ref[pair * K : (pair + 1) * K, side * K : (side + 1) * K] = grad
-    packed = pack(gram[:K, :K], gram[K:, K:])
-    query = query_ref[...]
+    query = query_ref[lax.axis_index("tensor")]
+    packed = pack(gram[:K, :K], gram[K:, K:], query)
+    for z in range(NZ):
+        send_ref[z] = packed
+
+
+def over_z_kernel(parts_ref, send_ref):
+    packed = added(parts_ref, pl.ds(0, GRAM))
+    queries = jnp.concatenate([parts_ref[z, GRAM - SLICE :] for z in range(NZ)], axis=0)
     for y in range(NY):
         send_ref[y, :GRAM] = packed
-        send_ref[y, GRAM:] = query
-
-
-def over_y_kernel(parts_ref, send_ref):
-    packed = added(parts_ref, pl.ds(0, GRAM))
-    for z in range(NZ):
-        send_ref[z] = packed
-
-
-def pack(square_in, square_out):
+        send_ref[y, GRAM:] = queries
+
+
+def pack(square_in, square_out, query):
     rows = lax.broadcasted_iota(jnp.int32, (K, K), 0)
     cols = lax.broadcasted_iota(jnp.int32, (K, K), 1)
     square = jnp.where(rows >= cols, square_in, square_out)
     diag = jnp.sum(jnp.where(rows == cols, square_out, 0.0), axis=0, keepdims=True)
-    diag = jnp.broadcast_to(jnp.concatenate([diag, diag], axis=1), (8, 2 * K))
+    diag = jnp.broadcast_to(jnp.concatenate([diag, diag], axis=1), (SLICE, 2 * K))
     return jnp.concatenate(
-        [jnp.concatenate([square[: K // 2], square[K // 2 :]], axis=1), diag], axis=0
+        [jnp.concatenate([square[: K // 2], square[K // 2 :]], axis=1), diag, query], axis=0
     )
 
 def unpack(packed):
@@ -168,17 +160,17 @@
     square_out = jnp.where(rows == cols, packed[K // 2 : K // 2 + 1, :K], square_out)
     return square_in, square_out
 
-def wide_rows(wide_ref):
+def wide_rows(wide_ref, count):
     blocks = []
     for pair in range(2):
-        even = wide_ref[pl.ds(pair * K, K // 2, stride=2), :]
-        odd = wide_ref[pl.ds(pair * K + 1, K // 2, stride=2), :]
+        even = wide_ref[pl.ds(pair * count, count // 2, stride=2), :]
+        odd = wide_ref[pl.ds(pair * count + 1, count // 2, stride=2), :]
         blocks.append(jnp.concatenate([even[:, :K], odd[:, :K]], axis=1))
         blocks.append(jnp.concatenate([even[:, K:], odd[:, K:]], axis=1))
     return blocks
 
 
-def tail_kernel(all_tokens, parts_ref, grads_ref, query_ref, factors_ref, send_ref, wide_ref):
+def tail_kernel(all_tokens, parts_ref, grads_ref, factors_ref, send_ref, inverse_ref, wide_ref):
     sum_in, sum_out = unpack(added(parts_ref, pl.ds(0, GRAM)))
     rows = lax.broadcasted_iota(jnp.int32, (K, 2 * K), 0)
     cols = lax.broadcasted_iota(jnp.int32, (K, 2 * K), 1)
@@ -186,38 +178,44 @@
     factors = jnp.concatenate([sum_in, sum_out], axis=1) / all_tokens + damping_level * eye_mats
     factors_ref[...] = factors
     inverse = gauss_jordan(factors, 8)
-    in_inv = inverse[:, :K]
+    inverse_ref[...] = inverse
+    count = 2 * SLICE
+    mine = inverse_ref[pl.ds(pl.multiple_of(lax.axis_index("tensor") * count, count), count), :]
     out_inv = inverse[:, K:] / float(K)
     zero = jnp.zeros((K, K), F32)
     pair_inv = jnp.concatenate(
         [jnp.concatenate([out_inv, zero], axis=1), jnp.concatenate([zero, out_inv], axis=1)], axis=0
     )
-    for pair in range(2):
-        left = jnp.dot(
-            in_inv, grads_ref[pair * K : (pair + 1) * K], precision=HI, preferred_element_type=F32
+    left = [
+        jnp.dot(
+            mine[:, :K],
+            grads_ref[pair * K : (pair + 1) * K],
+            precision=HI,
+            preferred_element_type=F32,
         )
-        wide_ref[pair * K : (pair + 1) * K] = jnp.dot(
-            left, pair_inv, precision=HI, preferred_element_type=F32
-        )
-    ready = wide_rows(wide_ref)
-    sums = [jnp.zeros((NY, 2 * K), F32) for _ in range(EX_DEV)]
-    for r in range(QROWS):
-        block = query_ref[pl.ds(GRAM + r, NY, stride=GRAM + QROWS), :]
+        for pair in range(2)
+    ]
+    wide_ref[...] = jnp.dot(
+        jnp.concatenate(left, axis=0), pair_inv, precision=HI, preferred_element_type=F32
+    )
+    ready = wide_rows(wide_ref, count)
+    sums = [[] for _ in range(EX_DEV)]
+    for y in range(NY):
+        blocks = [parts_ref[y, pl.ds(GRAM + r, NZ, stride=SLICE), :] for r in range(SLICE)]
         for e in range(EX_DEV):
-            sums[e] = sums[e] + block * ready[e][r : r + 1]
-    total = lax.dot_general(
+            total = blocks[0] * ready[e][:1]
+            for r in range(1, SLICE):
+                total = total + blocks[r] * ready[e][r : r + 1]
+            sums[e].append(total)
+    scores = lax.dot_general(
         jnp.ones((8, 2 * K), F32),
-        jnp.concatenate(sums, axis=0),
+        jnp.concatenate([total for part in sums for total in part], axis=0),
         (((1,), (1,)), ((), ())),
         precision=HI,
         preferred_element_type=F32,
     )
-    source = lax.broadcasted_iota(jnp.int32, (EX_DEV * NY, EX_DEV * NQ), 0)
-    target = lax.broadcasted_iota(jnp.int32, (EX_DEV * NY, EX_DEV * NQ), 1)
-    place = jnp.where(source * NZ + lax.axis_index("tensor") == target, 1.0, 0.0)
-    placed = jnp.dot(total, place, precision=HI, preferred_element_type=F32)
     for t in range(NT):
-        send_ref[t] = placed[:1]
+        send_ref[t] = scores[:1]
 
 
 def last_kernel(parts_ref, factors_ref, wide_ref, grads_ref, fin_ref, fout_ref, scores_ref, tall_ref):
@@ -226,7 +224,7 @@
         scores_ref[e : e + 1, :] = total[:, e * NQ : (e + 1) * NQ]
     fin_ref[...] = factors_ref[:, :K]
     fout_ref[...] = factors_ref[:, K:]
-    for e, block in enumerate(wide_rows(wide_ref)):
+    for e, block in enumerate(wide_rows(wide_ref, K)):
         tall_ref[e * QROWS : (e + 1) * QROWS] = block
     for r in range(QROWS):
         grads_ref[:, r * 2 * K : (r + 1) * 2 * K] = tall_ref[pl.ds(r, EX_DEV, stride=QROWS), :]
@@ -234,22 +232,25 @@
 
 def local(hidden_act, grad_out, proj_in, proj_out, queries):
     all_tokens = float(hidden_act.shape[0] * lax.axis_size("dp"))
-    query = lax.ppermute(queries.reshape(QROWS, 2 * K), ("dp", "tensor"), swap_pairs())
     part = project(hidden_act, grad_out, proj_in, proj_out)
     parts = lax.all_to_all(part, "tensor", 0, 0)
-    send, query = call(rows_kernel, [(NT, ROWS, 2 * K), (QROWS, 2 * K)], parts, query)
+    (send,) = call(rows_kernel, [(NT, ROWS, 2 * K)], parts)
     rows = lax.all_to_all(send, "tensor", 0, 0)
-    send, wide = call(gram_kernel, [(NY, GRAM + QROWS, 2 * K), (2 * K, 2 * K)], rows, query)
-    over_y = lax.all_to_all(send, "dp", 0, 0, axis_index_groups=Y_GROUPS)
-    (send,) = call(over_y_kernel, [(NZ, GRAM, 2 * K)], over_y)
+    send, wide = call(
+        gram_kernel,
+        [(NZ, GRAM, 2 * K), (2 * K, 2 * K)],
+        rows,
+        queries.reshape(NT, SLICE, 2 * K),
+    )
     parts = lax.all_to_all(send, "dp", 0, 0, axis_index_groups=Z_GROUPS)
+    (send,) = call(over_z_kernel, [(NY, GRAM + QROWS, 2 * K)], parts)
+    parts = lax.all_to_all(send, "dp", 0, 0, axis_index_groups=Y_GROUPS)
     factors, send = call(
         functools.partial(tail_kernel, all_tokens),
         [(K, 2 * K), (NT, 1, EX_DEV * NQ)],
         parts,
         wide,
-        over_y.reshape(NY * (GRAM + QROWS), 2 * K),
-        scratch=[(2 * K, 2 * K)],
+        scratch=[(K, 2 * K), (4 * SLICE, 2 * K)],
     )
     parts = lax.all_to_all(send, "tensor", 0, 0)
     return tuple(

time: 83.6 us -> 76.7 us (0.917)
  starting transfers between devices: 12.1 us -> 0 us
  blocking collectives: 57.3 us -> 66.9 us
  waiting for transfers between devices: 4.3 us -> 0 us
    all_to_all x1 -> x2, blocking collectives: 13.1 us -> 32.7 us  [the longest x1 16.4 us: local(): parts = lax.all_to_all(part, 'tensor', 0, 0)]
    all_to_all x1 -> x0, starting transfers between devices: 10.2 us -> none  [local(): parts = lax.all_to_all(part, 'tensor', 0, 0)]
    all_to_all x1, blocking collectives: 16.5 us -> 9.59 us  [local(): rows = lax.all_to_all(send, 'tensor', 0, 0)]
    ppermute x1 -> x0, waiting for transfers between devices: 3.42 us -> none  [local(): lax.ppermute(queries.reshape(QROWS, 2 * K), ('dp', 'tensor'), swap_pairs())]
    all_to_all x1, blocking collectives: 16.4 us -> 13.5 us  [local(): parts = lax.all_to_all(send, 'dp', 0, 0, axis_index_groups=Z_GROUPS)]
    ppermute x1 -> x0, starting transfers between devices: 1.91 us -> none  [local(): lax.ppermute(queries.reshape(QROWS, 2 * K), ('dp', 'tensor'), swap_pairs())]
    all_to_all x1 -> x0, waiting for transfers between devices: 0.87 us -> none  [local(): parts = lax.all_to_all(part, 'tensor', 0, 0)]
  transfers between devices with their start and end apart: 2 -> 0, of which waited for: 2 -> 0; matrix products, arithmetic and copies ran while one was open for 0% -> 0% of each run, Pallas kernels for 0% -> 0%
where the time goes in v3:
time: 76.7 us; the launch traced here: 76.3 us
  blocking collectives  66.9 us (87%)
  Pallas kernels  8.81 us (11%)
    all_to_all x1, blocking collectives, local(): parts = lax.all_to_all(part, 'tensor', 0, 0)  16.4 us
    all_to_all x1, blocking collectives, local(): parts = lax.all_to_all(send, 'dp', 0, 0, axis_index_groups=Y_GROUPS)  16.3 us
    all_to_all x1, blocking collectives, local(): parts = lax.all_to_all(send, 'dp', 0, 0, axis_index_groups=Z_GROUPS)  13.5 us
    all_to_all x1, blocking collectives, local(): parts = lax.all_to_all(send, 'tensor', 0, 0)  11.1 us
    all_to_all x1, blocking collectives, local(): rows = lax.all_to_all(send, 'tensor', 0, 0)  9.59 us
    pallas_call x5, Pallas kernels, call(): pl.pallas_call(body, out_shape=[jax.ShapeDtypeStruct(shape, F32) for shap...  4.64 us
    pallas_call x1, Pallas kernels, project(): pl.pallas_call(project_kernel, in_specs=[pl.BlockSpec(memory_space=pltpu....  4.17 us

profile of v3, /device:TPU:1, one launch (start us, length us, event | category | flops | bytes accessed | tf_op | source)
XLA Modules:
  0.0 76.3 jit_solution(15084206737658977529)
XLA Ops:
  0.6 0.0 copy-start
  0.6 4.2 %shard_map.84 = f32[8,56,128]{2,1,0:T(8,128)} custom-call(bf16[448,3584]{1,0:T(8,128)(2,1)} %hidden_ref.1, bf16[448,1024]{1,0:T(8,128)(2,1)} %grad_ref.1, bf16[64,3584]{1,0:T(8,128)(2,1)} %bitcast.4, bf16[64,1024]{1,0:T(8,128)(2,1)} %bitcast.5), custom_call_target="tpu_custom_call" | custom-call | tf_op jit(solution)/shard_map/pallas_call | solution.py:102
  4.8 16.4 %all_to_all.25.parts_ref = f32[8,56,128]{2,1,0:T(8,128)S(1)} all-to-all(f32[8,56,128]{2,1,0:T(8,128)} %shard_map.84), channel_id=1, replica_groups=mesh['dp'=64,'tensor'=8] {'tensor'}, dimensions={0} | all-to-all | bytes 458752 | tf_op jit(solution)/shard_map/all_to_all | solution.py:236
  21.2 9.6 %all_to_all.26.rows_ref = f32[8,56,128]{2,1,0:T(8,128)S(1)} all-to-all(f32[8,56,128]{2,1,0:T(8,128)S(1)} %shard_map.85), channel_id=1, replica_groups=mesh['dp'=64,'tensor'=8] {'tensor'}, dimensions={0} | all-to-all | bytes 458752 | tf_op jit(solution)/shard_map/all_to_all | solution.py:238
  30.8 0.0 copy-done
  30.8 0.6 shard_map.86
  31.4 13.5 %all_to_all.27.parts_ref = f32[8,40,128]{2,1,0:T(8,128)S(1)} all-to-all(f32[8,40,128]{2,1,0:T(8,128)S(1)} %get-tuple-element.8), channel_id=1, replica_groups={{0,8,16,24,32,40,48,56},{64,72,80,88,96,104,112,120},{128,136,144,152,1..., dimensions={0} | all-to-all | bytes 327680 | tf_op jit(solution)/shard_map/all_to_all | solution.py:245
  44.9 16.3 %all_to_all.28.parts_ref = f32[8,72,128]{2,1,0:T(8,128)S(1)} all-to-all(f32[8,72,128]{2,1,0:T(8,128)S(1)} %shard_map.87), channel_id=1, replica_groups={{0,64,128,192,256,320,384,448},{8,72,136,200,264,328,392,456},{16,80,14..., dimensions={0} | all-to-all | bytes 589824 | tf_op jit(solution)/shard_map/all_to_all | solution.py:247
  61.3 3.3 %shard_map.88 = (f32[64,128]{1,0:T(8,128)S(1)}, f32[8,1,256]{2,1,0:T(1,128)S(1)}) custom-call(f32[8,72,128]{2,1,0:T(8,128)S(1)} %all_to_all.28.parts_ref, f32[128,128]{1,0:T(8,128)S(1)} %get-tuple-element.9.grads_ref.wide_ref), custom_call_target="tpu_custom_call" | custom-call | flops 1048576 | bytes 1048576 | tf_op jit(solution)/shard_map/pallas_call | solution.py:55
  64.5 11.1 %all_to_all.29.parts_ref = f32[8,1,256]{2,1,0:T(1,128)S(1)} all-to-all(f32[8,1,256]{2,1,0:T(1,128)S(1)} %get-tuple-element.10), channel_id=1, replica_groups=mesh['dp'=64,'tensor'=8] {'tensor'}, dimensions={0} | all-to-all | bytes 16384 | tf_op jit(solution)/shard_map/all_to_all | solution.py:255
  75.6 0.8 shard_map.89
  (2 shorter events, 0.1 us)
Async XLA Ops:
  0.6 30.2 %copy-start = (f32[1,4096]{1,0:T(1,128)S(1)}, f32[1,4096]{1,0:T(1,128)}, u32[]{:S(2)}) copy-start(f32[1,4096]{1,0:T(1,128)} %param.9) | copy-start | bytes 49156

commit v4 on v3

--- a/solution.py
+++ b/solution.py
@@ -32,23 +32,47 @@
 Z_GROUPS = [[y * NZ + z for z in range(NZ)] for y in range(NY)]
 
 
-def gauss_jordan(m, panel):
-    lane = lax.broadcasted_iota(jnp.int32, (K, 2 * K), 1)
+def ldl_inverse(m):
+    count = K // 8
+    tiles = [m[8 * i : 8 * i + 8] for i in range(count)]
+    lane = lax.broadcasted_iota(jnp.int32, (8, 2 * K), 1)
     half = lane & K
     col_of = lane & (K - 1)
-    sub = lax.broadcasted_iota(jnp.int32, (K, 2 * K), 0)
-    for first in range(0, K, panel):
-        cols = [jnp.take_along_axis(m, half + k, axis=1) for k in range(first, first + panel)]
-        for k in range(first, first + panel):
-            c = cols[k - first]
-            inv = 1.0 / c[k : k + 1]
-            row = jnp.where(col_of[:1] == k, 1.0, m[k : k + 1]) * inv
-            for j in range(k + 1, first + panel):
-                d = cols[j - first]
-                f = d[k : k + 1] * inv
-                cols[j - first] = jnp.where(sub == k, f, d - c * f)
-            m = jnp.where(sub == k, row, jnp.where(col_of == k, 0.0, m) - c * row)
-    return m
+    sub = lax.broadcasted_iota(jnp.int32, (8, 2 * K), 0)
+    unit, scaled = [], []
+    for p in range(count):
+        below = range(p, count)
+        cols = [
+            {t: jnp.take_along_axis(tiles[t], half + (8 * p + s), axis=1) for t in below}
+            for s in range(8)
+        ]
+        inside = (col_of & -8) == 8 * p
+        for t in below:
+            tiles[t] = jnp.where(inside, 0.0, tiles[t])
+        inverses = []
+        for s in range(8):
+            c = cols[s]
+            inv = 1.0 / c[p][s : s + 1]
+            inverses.append(inv)
+            for j in range(s + 1, 8):
+                d = cols[j]
+                f = d[p][s : s + 1] * inv
+                cols[j] = {t: d[t] - c[t] * f for t in below}
+            row = jnp.where(col_of[:1] == 8 * p + s, 1.0, tiles[p][s : s + 1]) * inv
+            for t in below:
+                new = tiles[t] - c[t] * row
+                tiles[t] = jnp.where(sub > s, new, tiles[t]) if t == p else new
+        lower = jnp.where(col_of < 8 * p + sub, tiles[p], jnp.where(col_of == 8 * p + sub, 1.0, 0.0))
+        unit.append(lower)
+        scaled.append(lower * jnp.concatenate(inverses, axis=0))
+    both = lax.dot_general(
+        jnp.concatenate(unit, axis=0),
+        jnp.concatenate(scaled, axis=0),
+        (((0,), (0,)), ((), ())),
+        precision=HI,
+        preferred_element_type=F32,
+    )
+    return jnp.concatenate([both[:K, :K], both[K:, K:]], axis=1)
 
 
 def call(body, outs, *args, scratch=(), flops=1 << 20):
@@ -86,15 +110,14 @@
         first += size
     wout_copy.wait()
     grad_copy.wait()
-    out_part = lax.dot_general(grad[...], wout[...], contract, preferred_element_type=F32)
+    out_part = lax.dot_general(wout[...], grad[...], contract, preferred_element_type=F32)
     win_copy.wait()
     in_part = None
     for copy, units in blocks:
         copy.wait()
-        part = lax.dot_general(hidden[:, units], win[:, units], contract, preferred_element_type=F32)
+        part = lax.dot_general(win[:, units], hidden[:, units], contract, preferred_element_type=F32)
         in_part = part if in_part is None else in_part + part
-    out_ref[:, :, :K] = in_part.reshape(NT, ROWS, K)
-    out_ref[:, :, K:] = out_part.reshape(NT, ROWS, K)
+    out_ref[...] = jnp.concatenate([in_part, out_part], axis=0).T.reshape(NT, ROWS, 2 * K)
 
 
 def project(hidden_act, grad_out, proj_in, proj_out):
@@ -177,7 +200,7 @@
     eye_mats = jnp.where(rows == (cols & (K - 1)), 1.0, 0.0)
     factors = jnp.concatenate([sum_in, sum_out], axis=1) / all_tokens + damping_level * eye_mats
     factors_ref[...] = factors
-    inverse = gauss_jordan(factors, 8)
+    inverse = ldl_inverse(factors)
     inverse_ref[...] = inverse
     count = 2 * SLICE
     mine = inverse_ref[pl.ds(pl.multiple_of(lax.axis_index("tensor") * count, count), count), :]

time: 76.7 us -> 76.2 us (level)
  no operation moved by 1% of the time
where the time goes in v4:
time: 76.2 us; the launch traced here: 75.9 us
  blocking collectives  66.9 us (88%)
  Pallas kernels  8.37 us (11%)
    all_to_all x1, blocking collectives, local(): parts = lax.all_to_all(part, 'tensor', 0, 0)  16.4 us
    all_to_all x1, blocking collectives, local(): parts = lax.all_to_all(send, 'dp', 0, 0, axis_index_groups=Y_GROUPS)  16.3 us
    all_to_all x1, blocking collectives, local(): parts = lax.all_to_all(send, 'dp', 0, 0, axis_index_groups=Z_GROUPS)  13.5 us
    all_to_all x1, blocking collectives, local(): parts = lax.all_to_all(send, 'tensor', 0, 0)  11.1 us
    all_to_all x1, blocking collectives, local(): rows = lax.all_to_all(send, 'tensor', 0, 0)  9.59 us
    pallas_call x5, Pallas kernels, call(): pl.pallas_call(body, out_shape=[jax.ShapeDtypeStruct(shape, F32) for shap...  4.32 us
    pallas_call x1, Pallas kernels, project(): pl.pallas_call(project_kernel, in_specs=[pl.BlockSpec(memory_space=pltpu....  4.06 us

profile of v4, /device:TPU:1, one launch (start us, length us, event | category | flops | bytes accessed | tf_op | source)
XLA Modules:
  0.0 75.9 jit_solution(3697636232612595133)
XLA Ops:
  0.6 0.0 copy-start
  0.6 4.1 %shard_map.84 = f32[8,56,128]{2,1,0:T(8,128)} custom-call(bf16[448,3584]{1,0:T(8,128)(2,1)} %hidden_ref.1, bf16[448,1024]{1,0:T(8,128)(2,1)} %grad_ref.1, bf16[64,3584]{1,0:T(8,128)(2,1)} %bitcast.4, bf16[64,1024]{1,0:T(8,128)(2,1)} %bitcast.5), custom_call_target="tpu_custom_call" | custom-call | tf_op jit(solution)/shard_map/pallas_call | solution.py:125
  4.7 16.4 %all_to_all.25.parts_ref = f32[8,56,128]{2,1,0:T(8,128)S(1)} all-to-all(f32[8,56,128]{2,1,0:T(8,128)} %shard_map.84), channel_id=1, replica_groups=mesh['dp'=64,'tensor'=8] {'tensor'}, dimensions={0} | all-to-all | bytes 458752 | tf_op jit(solution)/shard_map/all_to_all | solution.py:259
  21.1 9.6 %all_to_all.26.rows_ref = f32[8,56,128]{2,1,0:T(8,128)S(1)} all-to-all(f32[8,56,128]{2,1,0:T(8,128)S(1)} %shard_map.85), channel_id=1, replica_groups=mesh['dp'=64,'tensor'=8] {'tensor'}, dimensions={0} | all-to-all | bytes 458752 | tf_op jit(solution)/shard_map/all_to_all | solution.py:261
  30.7 0.0 copy-done
  30.7 0.6 shard_map.86
  31.3 13.5 %all_to_all.27.parts_ref = f32[8,40,128]{2,1,0:T(8,128)S(1)} all-to-all(f32[8,40,128]{2,1,0:T(8,128)S(1)} %get-tuple-element.8), channel_id=1, replica_groups={{0,8,16,24,32,40,48,56},{64,72,80,88,96,104,112,120},{128,136,144,152,1..., dimensions={0} | all-to-all | bytes 327680 | tf_op jit(solution)/shard_map/all_to_all | solution.py:268
  44.8 16.3 %all_to_all.28.parts_ref = f32[8,72,128]{2,1,0:T(8,128)S(1)} all-to-all(f32[8,72,128]{2,1,0:T(8,128)S(1)} %shard_map.87), channel_id=1, replica_groups={{0,64,128,192,256,320,384,448},{8,72,136,200,264,328,392,456},{16,80,14..., dimensions={0} | all-to-all | bytes 589824 | tf_op jit(solution)/shard_map/all_to_all | solution.py:270
  61.1 2.9 %shard_map.88 = (f32[64,128]{1,0:T(8,128)S(1)}, f32[8,1,256]{2,1,0:T(1,128)S(1)}) custom-call(f32[8,72,128]{2,1,0:T(8,128)S(1)} %all_to_all.28.parts_ref, f32[128,128]{1,0:T(8,128)S(1)} %get-tuple-element.9.grads_ref.wide_ref), custom_call_target="tpu_custom_call" | custom-call | flops 1048576 | bytes 1048576 | tf_op jit(solution)/shard_map/pallas_call | solution.py:79
  64.1 11.1 %all_to_all.29.parts_ref = f32[8,1,256]{2,1,0:T(1,128)S(1)} all-to-all(f32[8,1,256]{2,1,0:T(1,128)S(1)} %get-tuple-element.10), channel_id=1, replica_groups=mesh['dp'=64,'tensor'=8] {'tensor'}, dimensions={0} | all-to-all | bytes 16384 | tf_op jit(solution)/shard_map/all_to_all | solution.py:278
  75.1 0.8 shard_map.89
  (2 shorter events, 0.1 us)
Async XLA Ops:
  0.6 30.1 %copy-start = (f32[1,4096]{1,0:T(1,128)S(1)}, f32[1,4096]{1,0:T(1,128)}, u32[]{:S(2)}) copy-start(f32[1,4096]{1,0:T(1,128)} %param.9) | copy-start | bytes 49156

commit v5 on v4

--- a/solution.py
+++ b/solution.py
@@ -19,7 +19,7 @@
 ROWS = 56
 QROWS = 32
 SLICE = QROWS // NT
-UNIT_BLOCKS = (1280, 1280, 1024)
+UNIT_BLOCKS = (512,) * 7
 HI = lax.Precision.HIGHEST
 F32 = jnp.float32
 VMEM_LIMIT = 16 << 20

time: 76.2 us -> 76 us (level)
  no operation moved by 1% of the time
where the time goes in v5:
time: 76 us; the launch traced here: 75.7 us
  blocking collectives  66.9 us (88%)
  Pallas kernels  8.14 us (11%)
    all_to_all x1, blocking collectives, local(): parts = lax.all_to_all(part, 'tensor', 0, 0)  16.4 us
    all_to_all x1, blocking collectives, local(): parts = lax.all_to_all(send, 'dp', 0, 0, axis_index_groups=Y_GROUPS)  16.3 us
    all_to_all x1, blocking collectives, local(): parts = lax.all_to_all(send, 'dp', 0, 0, axis_index_groups=Z_GROUPS)  13.5 us
    all_to_all x1, blocking collectives, local(): parts = lax.all_to_all(send, 'tensor', 0, 0)  11.1 us
    all_to_all x1, blocking collectives, local(): rows = lax.all_to_all(send, 'tensor', 0, 0)  9.59 us
    pallas_call x5, Pallas kernels, call(): pl.pallas_call(body, out_shape=[jax.ShapeDtypeStruct(shape, F32) for shap...  4.32 us
    pallas_call x1, Pallas kernels, project(): pl.pallas_call(project_kernel, in_specs=[pl.BlockSpec(memory_space=pltpu....  3.82 us

profile of v5, /device:TPU:1, one launch (start us, length us, event | category | flops | bytes accessed | tf_op | source)
XLA Modules:
  0.0 75.7 jit_solution(13589985206383761302)
XLA Ops:
  0.6 0.0 copy-start
  0.6 3.8 %shard_map.84 = f32[8,56,128]{2,1,0:T(8,128)} custom-call(bf16[448,3584]{1,0:T(8,128)(2,1)} %hidden_ref.1, bf16[448,1024]{1,0:T(8,128)(2,1)} %grad_ref.1, bf16[64,3584]{1,0:T(8,128)(2,1)} %bitcast.4, bf16[64,1024]{1,0:T(8,128)(2,1)} %bitcast.5), custom_call_target="tpu_custom_call" | custom-call | tf_op jit(solution)/shard_map/pallas_call | solution.py:125
  4.5 16.4 %all_to_all.25.parts_ref = f32[8,56,128]{2,1,0:T(8,128)S(1)} all-to-all(f32[8,56,128]{2,1,0:T(8,128)} %shard_map.84), channel_id=1, replica_groups=mesh['dp'=64,'tensor'=8] {'tensor'}, dimensions={0} | all-to-all | bytes 458752 | tf_op jit(solution)/shard_map/all_to_all | solution.py:259
  20.9 9.6 %all_to_all.26.rows_ref = f32[8,56,128]{2,1,0:T(8,128)S(1)} all-to-all(f32[8,56,128]{2,1,0:T(8,128)S(1)} %shard_map.85), channel_id=1, replica_groups=mesh['dp'=64,'tensor'=8] {'tensor'}, dimensions={0} | all-to-all | bytes 458752 | tf_op jit(solution)/shard_map/all_to_all | solution.py:261
  30.5 0.0 copy-done
  30.5 0.6 shard_map.86
  31.0 13.5 %all_to_all.27.parts_ref = f32[8,40,128]{2,1,0:T(8,128)S(1)} all-to-all(f32[8,40,128]{2,1,0:T(8,128)S(1)} %get-tuple-element.8), channel_id=1, replica_groups={{0,8,16,24,32,40,48,56},{64,72,80,88,96,104,112,120},{128,136,144,152,1..., dimensions={0} | all-to-all | bytes 327680 | tf_op jit(solution)/shard_map/all_to_all | solution.py:268
  44.6 16.3 %all_to_all.28.parts_ref = f32[8,72,128]{2,1,0:T(8,128)S(1)} all-to-all(f32[8,72,128]{2,1,0:T(8,128)S(1)} %shard_map.87), channel_id=1, replica_groups={{0,64,128,192,256,320,384,448},{8,72,136,200,264,328,392,456},{16,80,14..., dimensions={0} | all-to-all | bytes 589824 | tf_op jit(solution)/shard_map/all_to_all | solution.py:270
  60.9 2.9 %shard_map.88 = (f32[64,128]{1,0:T(8,128)S(1)}, f32[8,1,256]{2,1,0:T(1,128)S(1)}) custom-call(f32[8,72,128]{2,1,0:T(8,128)S(1)} %all_to_all.28.parts_ref, f32[128,128]{1,0:T(8,128)S(1)} %get-tuple-element.9.grads_ref.wide_ref), custom_call_target="tpu_custom_call" | custom-call | flops 1048576 | bytes 1048576 | tf_op jit(solution)/shard_map/pallas_call | solution.py:79
  63.8 11.1 %all_to_all.29.parts_ref = f32[8,1,256]{2,1,0:T(1,128)S(1)} all-to-all(f32[8,1,256]{2,1,0:T(1,128)S(1)} %get-tuple-element.10), channel_id=1, replica_groups=mesh['dp'=64,'tensor'=8] {'tensor'}, dimensions={0} | all-to-all | bytes 16384 | tf_op jit(solution)/shard_map/all_to_all | solution.py:278
  74.9 0.8 shard_map.89
  (2 shorter events, 0.1 us)
Async XLA Ops:
  0.6 29.8 %copy-start = (f32[1,4096]{1,0:T(1,128)S(1)}, f32[1,4096]{1,0:T(1,128)}, u32[]{:S(2)}) copy-start(f32[1,4096]{1,0:T(1,128)} %param.9) | copy-start | bytes 49156

commit v6 on v5

--- a/solution.py
+++ b/solution.py
@@ -19,7 +19,7 @@
 ROWS = 56
 QROWS = 32
 SLICE = QROWS // NT
-UNIT_BLOCKS = (512,) * 7
+UNIT_BLOCKS = (1024, 1024, 1024, 512)
 HI = lax.Precision.HIGHEST
 F32 = jnp.float32
 VMEM_LIMIT = 16 << 20
@@ -75,6 +75,14 @@
     return jnp.concatenate([both[:K, :K], both[K:, K:]], axis=1)
 
 
+def split(x):
+    parts = []
+    for _ in range(3):
+        parts.append(x.astype(jnp.bfloat16))
+        x = x - parts[-1].astype(F32)
+    return parts
+
+
 def call(body, outs, *args, scratch=(), flops=1 << 20):
     return pl.pallas_call(
         body,
@@ -230,13 +238,13 @@
             for r in range(1, SLICE):
                 total = total + blocks[r] * ready[e][r : r + 1]
             sums[e].append(total)
-    scores = lax.dot_general(
-        jnp.ones((8, 2 * K), F32),
-        jnp.concatenate([total for part in sums for total in part], axis=0),
-        (((1,), (1,)), ((), ())),
-        precision=HI,
-        preferred_element_type=F32,
-    )
+    totals = split(jnp.concatenate([total for part in sums for total in part], axis=0))
+    ones = jnp.ones((8, 2 * K), jnp.bfloat16)
+    scores = [
+        lax.dot_general(ones, x, (((1,), (1,)), ((), ())), preferred_element_type=F32)
+        for x in totals
+    ]
+    scores = scores[0] + (scores[1] + scores[2])
     for t in range(NT):
         send_ref[t] = scores[:1]
 

time: 76 us -> 76.1 us (level)
  no operation moved by 1% of the time
where the time goes in v6:
time: 76.1 us; the launch traced here: 75.7 us
  blocking collectives  66.9 us (88%)
  Pallas kernels  8.19 us (11%)
    all_to_all x1, blocking collectives, local(): parts = lax.all_to_all(part, 'tensor', 0, 0)  16.4 us
    all_to_all x1, blocking collectives, local(): parts = lax.all_to_all(send, 'dp', 0, 0, axis_index_groups=Y_GROUPS)  16.3 us
    all_to_all x1, blocking collectives, local(): parts = lax.all_to_all(send, 'dp', 0, 0, axis_index_groups=Z_GROUPS)  13.5 us
    all_to_all x1, blocking collectives, local(): parts = lax.all_to_all(send, 'tensor', 0, 0)  11.1 us
    all_to_all x1, blocking collectives, local(): rows = lax.all_to_all(send, 'tensor', 0, 0)  9.59 us
    pallas_call x5, Pallas kernels, call(): pl.pallas_call(body, out_shape=[jax.ShapeDtypeStruct(shape, F32) for shap...  4.26 us
    pallas_call x1, Pallas kernels, project(): pl.pallas_call(project_kernel, in_specs=[pl.BlockSpec(memory_space=pltpu....  3.93 us

profile of v6, /device:TPU:1, one launch (start us, length us, event | category | flops | bytes accessed | tf_op | source)
XLA Modules:
  0.0 75.7 jit_solution(7545387928428001632)
XLA Ops:
  0.6 0.0 copy-start
  0.6 3.9 %shard_map.84 = f32[8,56,128]{2,1,0:T(8,128)} custom-call(bf16[448,3584]{1,0:T(8,128)(2,1)} %hidden_ref.1, bf16[448,1024]{1,0:T(8,128)(2,1)} %grad_ref.1, bf16[64,3584]{1,0:T(8,128)(2,1)} %bitcast.4, bf16[64,1024]{1,0:T(8,128)(2,1)} %bitcast.5), custom_call_target="tpu_custom_call" | custom-call | tf_op jit(solution)/shard_map/pallas_call | solution.py:133
  4.6 16.4 %all_to_all.25.parts_ref = f32[8,56,128]{2,1,0:T(8,128)S(1)} all-to-all(f32[8,56,128]{2,1,0:T(8,128)} %shard_map.84), channel_id=1, replica_groups=mesh['dp'=64,'tensor'=8] {'tensor'}, dimensions={0} | all-to-all | bytes 458752 | tf_op jit(solution)/shard_map/all_to_all | solution.py:267
  21.0 9.6 %all_to_all.26.rows_ref = f32[8,56,128]{2,1,0:T(8,128)S(1)} all-to-all(f32[8,56,128]{2,1,0:T(8,128)S(1)} %shard_map.85), channel_id=1, replica_groups=mesh['dp'=64,'tensor'=8] {'tensor'}, dimensions={0} | all-to-all | bytes 458752 | tf_op jit(solution)/shard_map/all_to_all | solution.py:269
  30.6 0.0 copy-done
  30.6 0.6 shard_map.86
  31.2 13.5 %all_to_all.27.parts_ref = f32[8,40,128]{2,1,0:T(8,128)S(1)} all-to-all(f32[8,40,128]{2,1,0:T(8,128)S(1)} %get-tuple-element.8), channel_id=1, replica_groups={{0,8,16,24,32,40,48,56},{64,72,80,88,96,104,112,120},{128,136,144,152,1..., dimensions={0} | all-to-all | bytes 327680 | tf_op jit(solution)/shard_map/all_to_all | solution.py:276
  44.7 16.3 %all_to_all.28.parts_ref = f32[8,72,128]{2,1,0:T(8,128)S(1)} all-to-all(f32[8,72,128]{2,1,0:T(8,128)S(1)} %shard_map.87), channel_id=1, replica_groups={{0,64,128,192,256,320,384,448},{8,72,136,200,264,328,392,456},{16,80,14..., dimensions={0} | all-to-all | bytes 589824 | tf_op jit(solution)/shard_map/all_to_all | solution.py:278
  61.0 2.9 %shard_map.88 = (f32[64,128]{1,0:T(8,128)S(1)}, f32[8,1,256]{2,1,0:T(1,128)S(1)}) custom-call(f32[8,72,128]{2,1,0:T(8,128)S(1)} %all_to_all.28.parts_ref, f32[128,128]{1,0:T(8,128)S(1)} %get-tuple-element.9.grads_ref.wide_ref), custom_call_target="tpu_custom_call" | custom-call | flops 1048576 | bytes 1048576 | tf_op jit(solution)/shard_map/pallas_call | solution.py:87
  63.9 11.1 %all_to_all.29.parts_ref = f32[8,1,256]{2,1,0:T(1,128)S(1)} all-to-all(f32[8,1,256]{2,1,0:T(1,128)S(1)} %get-tuple-element.10), channel_id=1, replica_groups=mesh['dp'=64,'tensor'=8] {'tensor'}, dimensions={0} | all-to-all | bytes 16384 | tf_op jit(solution)/shard_map/all_to_all | solution.py:286
  75.0 0.8 shard_map.89
  (2 shorter events, 0.1 us)
Async XLA Ops:
  0.6 30.0 %copy-start = (f32[1,4096]{1,0:T(1,128)S(1)}, f32[1,4096]{1,0:T(1,128)}, u32[]{:S(2)}) copy-start(f32[1,4096]{1,0:T(1,128)} %param.9) | copy-start | bytes 49156

commit v7 on v6

--- a/solution.py
+++ b/solution.py
@@ -217,15 +217,9 @@
     pair_inv = jnp.concatenate(
         [jnp.concatenate([out_inv, zero], axis=1), jnp.concatenate([zero, out_inv], axis=1)], axis=0
     )
-    left = [
-        jnp.dot(
-            mine[:, :K],
-            grads_ref[pair * K : (pair + 1) * K],
-            precision=HI,
-            preferred_element_type=F32,
-        )
-        for pair in range(2)
-    ]
+    grads = jnp.concatenate([grads_ref[:K], grads_ref[K:]], axis=1)
+    left = jnp.dot(mine[:, :K], grads, precision=HI, preferred_element_type=F32)
+    left = [left[:, : 2 * K], left[:, 2 * K :]]
     wide_ref[...] = jnp.dot(
         jnp.concatenate(left, axis=0), pair_inv, precision=HI, preferred_element_type=F32
     )

time: 76.1 us -> 76 us (level)
  no operation moved by 1% of the time
where the time goes in v7:
time: 76 us; the launch traced here: 75.7 us
  blocking collectives  66.9 us (88%)
  Pallas kernels  8.11 us (11%)
    all_to_all x1, blocking collectives, local(): parts = lax.all_to_all(part, 'tensor', 0, 0)  16.4 us
    all_to_all x1, blocking collectives, local(): parts = lax.all_to_all(send, 'dp', 0, 0, axis_index_groups=Y_GROUPS)  16.3 us
    all_to_all x1, blocking collectives, local(): parts = lax.all_to_all(send, 'dp', 0, 0, axis_index_groups=Z_GROUPS)  13.5 us
    all_to_all x1, blocking collectives, local(): parts = lax.all_to_all(send, 'tensor', 0, 0)  11.1 us
    all_to_all x1, blocking collectives, local(): rows = lax.all_to_all(send, 'tensor', 0, 0)  9.59 us
    pallas_call x5, Pallas kernels, call(): pl.pallas_call(body, out_shape=[jax.ShapeDtypeStruct(shape, F32) for shap...  4.18 us
    pallas_call x1, Pallas kernels, project(): pl.pallas_call(project_kernel, in_specs=[pl.BlockSpec(memory_space=pltpu....  3.93 us

profile of v7, /device:TPU:1, one launch (start us, length us, event | category | flops | bytes accessed | tf_op | source)
XLA Modules:
  0.0 75.7 jit_solution(4761253880574126002)
XLA Ops:
  0.6 0.0 copy-start
  0.6 3.9 %shard_map.84 = f32[8,56,128]{2,1,0:T(8,128)} custom-call(bf16[448,3584]{1,0:T(8,128)(2,1)} %hidden_ref.1, bf16[448,1024]{1,0:T(8,128)(2,1)} %grad_ref.1, bf16[64,3584]{1,0:T(8,128)(2,1)} %bitcast.4, bf16[64,1024]{1,0:T(8,128)(2,1)} %bitcast.5), custom_call_target="tpu_custom_call" | custom-call | tf_op jit(solution)/shard_map/pallas_call | solution.py:133
  4.6 16.4 %all_to_all.25.parts_ref = f32[8,56,128]{2,1,0:T(8,128)S(1)} all-to-all(f32[8,56,128]{2,1,0:T(8,128)} %shard_map.84), channel_id=1, replica_groups=mesh['dp'=64,'tensor'=8] {'tensor'}, dimensions={0} | all-to-all | bytes 458752 | tf_op jit(solution)/shard_map/all_to_all | solution.py:261
  21.0 9.6 %all_to_all.26.rows_ref = f32[8,56,128]{2,1,0:T(8,128)S(1)} all-to-all(f32[8,56,128]{2,1,0:T(8,128)S(1)} %shard_map.85), channel_id=1, replica_groups=mesh['dp'=64,'tensor'=8] {'tensor'}, dimensions={0} | all-to-all | bytes 458752 | tf_op jit(solution)/shard_map/all_to_all | solution.py:263
  30.6 0.0 copy-done
  30.6 0.6 shard_map.86
  31.2 13.5 %all_to_all.27.parts_ref = f32[8,40,128]{2,1,0:T(8,128)S(1)} all-to-all(f32[8,40,128]{2,1,0:T(8,128)S(1)} %get-tuple-element.8), channel_id=1, replica_groups={{0,8,16,24,32,40,48,56},{64,72,80,88,96,104,112,120},{128,136,144,152,1..., dimensions={0} | all-to-all | bytes 327680 | tf_op jit(solution)/shard_map/all_to_all | solution.py:270
  44.7 16.3 %all_to_all.28.parts_ref = f32[8,72,128]{2,1,0:T(8,128)S(1)} all-to-all(f32[8,72,128]{2,1,0:T(8,128)S(1)} %shard_map.87), channel_id=1, replica_groups={{0,64,128,192,256,320,384,448},{8,72,136,200,264,328,392,456},{16,80,14..., dimensions={0} | all-to-all | bytes 589824 | tf_op jit(solution)/shard_map/all_to_all | solution.py:272
  61.0 2.8 %shard_map.88 = (f32[64,128]{1,0:T(8,128)S(1)}, f32[8,1,256]{2,1,0:T(1,128)S(1)}) custom-call(f32[8,72,128]{2,1,0:T(8,128)S(1)} %all_to_all.28.parts_ref, f32[128,128]{1,0:T(8,128)S(1)} %get-tuple-element.9.grads_ref.wide_ref), custom_call_target="tpu_custom_call" | custom-call | flops 1048576 | bytes 1048576 | tf_op jit(solution)/shard_map/pallas_call | solution.py:87
  63.8 11.1 %all_to_all.29.parts_ref = f32[8,1,256]{2,1,0:T(1,128)S(1)} all-to-all(f32[8,1,256]{2,1,0:T(1,128)S(1)} %get-tuple-element.10), channel_id=1, replica_groups=mesh['dp'=64,'tensor'=8] {'tensor'}, dimensions={0} | all-to-all | bytes 16384 | tf_op jit(solution)/shard_map/all_to_all | solution.py:280
  74.9 0.8 shard_map.89
  (2 shorter events, 0.1 us)
Async XLA Ops:
  0.6 30.0 %copy-start = (f32[1,4096]{1,0:T(1,128)S(1)}, f32[1,4096]{1,0:T(1,128)}, u32[]{:S(2)}) copy-start(f32[1,4096]{1,0:T(1,128)} %param.9) | copy-start | bytes 49156
